TPU v7x, 256 devices: a whole 4x4x8 slice. The times are simulated.
256 devices in a mesh: lon: 128 (over z, y, x_hi, core), lat: 2 (over x_lo).
Axes of the slice: x: 4 (x_hi: 2, x_lo: 2; x = x_hi * 2 + x_lo), y: 4, z: 8, core: 2. Of those that a mesh axis runs over, the one named last changes fastest.
Arguments:
- tokens: bfloat16 [48, 1536, 2, 1024], P('lat', 'lon'), may hold values from -420 to 420
- land_mask: int32 [48, 1536], P('lat', 'lon'), may hold values from 0 to 1
- land_bias: float32 [8], replicated, may hold values from -300 to 300
- qkv_weight: bfloat16 [1024, 1536], replicated, may hold values from -0.1875 to 0.1875
- out_weight: bfloat16 [512, 1024], replicated, may hold values from -0.25 to 0.25
- cotangent: bfloat16 [48, 1536, 2, 1024], P('lat', 'lon'), may hold values from -24 to 24
Outputs:
- block_out: bfloat16 [48, 1536, 2, 1024], P('lat', 'lon')
- grad_tokens: bfloat16 [48, 1536, 2, 1024], P('lat', 'lon')
- grad_qkv: float32 [1024, 1536], P('lon')
- grad_out: float32 [512, 1024], P(None, 'lon')
All inputs are finite; a program needn't handle non-finite values.
Results may differ from a plain program's by a relative error of at most 0.012.
Values may be sent and summed in bfloat16 or wider, within the bound.
No kernel may reach another device: no remote copies, remote signals or barrier semaphores. Data moves between devices by JAX's collectives and lax.ppermute only.
A program may use at most 128 MiB of HBM per device.

v0:
```python
import math

import jax
import jax.numpy as jnp
import numpy as np
from jax import lax
from jax.experimental import pallas as pl
from jax.experimental.pallas import tpu as pltpu
from jax.sharding import Mesh, PartitionSpec as P

D = 1024
HEADS = 8
HSIZE = 64
HD = 512
WIN = 144
HALF = 72
WINS = 4
TOK = 576
SLAB = 128
TOKENS = 147456
GRAD_SCALE = 1.0 / math.sqrt(TOKENS)
FACTOR = HSIZE ** (-0.5)
FAR = -1e30
BF = jnp.bfloat16
F32 = jnp.float32
LON = ("z", "y", "xh", "core")
ALL = LON + ("lat",)
SIZES = (8, 4, 2, 2, 2)
PEERS = ((0, 1), (1, 0), (1, 1))


def nn(a, b):
    return lax.dot_general(a, b, (((1,), (0,)), ((), ())), preferred_element_type=F32)


def nt(a, b):
    return lax.dot_general(a, b, (((1,), (1,)), ((), ())), preferred_element_type=F32)


def tn(a, b):
    return lax.dot_general(a, b, (((0,), (0,)), ((), ())), preferred_element_type=F32)


def window_rows(own, main, lat, diag, w):
    if w < WINS - 1:
        parts = [own[3 + 6 * w : 9 + 6 * w, 6:12], main[6 * w : 6 * w + 6]]
    else:
        parts = [own[21:24, 6:12], lat[0:3], main[18:21], diag[0:3]]
    return jnp.concatenate([p.astype(F32).reshape(-1, D) for p in parts], 0)


def halo_copies(block, main, lat, diag, sems):
    return [
        pltpu.make_async_copy(block.at[3:10, 0:6], main.at[0:7], sems.at[0]),
        pltpu.make_async_copy(block.at[10:17, 0:6], main.at[7:14], sems.at[1]),
        pltpu.make_async_copy(block.at[17:24, 0:6], main.at[14:21], sems.at[2]),
        pltpu.make_async_copy(block.at[0:3, 6:12], lat.at[0:3], sems.at[3]),
        pltpu.make_async_copy(block.at[0:3, 0:6], diag.at[0:3], sems.at[4]),
    ]


def tok_halo_kernel(land, tok, main, lat, diag, main_v, lat_v, diag_v, sems):
    copies = halo_copies(tok, main_v, lat_v, diag_v, sems.at[0])
    for c in copies:
        c.start()
    by_row = jnp.concatenate([land[...].astype(F32), jnp.zeros((12, D - 24), F32)], 1)
    cells = jnp.broadcast_to(by_row[:, None, :], (12, 2, D)).astype(BF)
    main_v[21] = cells[0:6]
    lat_v[3] = cells[6:12]
    diag_v[3] = cells[0:6]
    done = []
    for i, (rows, wide, ref) in enumerate(
        (((0, 7), main_v, main), ((7, 14), main_v, main), ((14, 22), main_v, main),
         ((0, 4), lat_v, lat), ((0, 4), diag_v, diag))
    ):
        copies[i].wait()
        rows = slice(*rows)
        done.append(pltpu.make_async_copy(wide.at[rows], ref.at[rows], sems.at[1, i]))
        done[-1].start()
    for c in done:
        c.wait()


def cot_halo_kernel(cot, main, lat, diag, sems):
    copies = halo_copies(cot, main, lat, diag, sems)
    for c in copies:
        c.start()
    for c in copies:
        c.wait()


def weights_kernel(wqkv_hbm, wout_hbm, wqkv, wout, sems):
    copies = [pltpu.make_async_copy(wout_hbm, wout, sems.at[4])]
    for i in range(4):
        rows = slice(256 * i, 256 * i + 256)
        copies.append(pltpu.make_async_copy(wqkv_hbm.at[rows], wqkv.at[rows], sems.at[i]))
    for c in copies:
        c.start()
    for c in copies:
        c.wait()


def land_column(cells, first_row, rows):
    count = rows * 12
    token = lax.broadcasted_iota(jnp.int32, (count, 128), 0)
    lane = lax.broadcasted_iota(jnp.int32, (count, 128), 1)
    cell = lax.broadcasted_iota(jnp.int32, (count, 12), 0) % 12
    pick = (cell == lax.broadcasted_iota(jnp.int32, (count, 12), 1)).astype(F32)
    wide = nn(pick, cells)
    return jnp.sum(jnp.where(lane == token // 12 + first_row, wide, 0.0), 1, keepdims=True)


def forward_kernel(
    bias, tok, main, lat, diag, land, wqkv,
    nrm, inv_s, qkv, attn_s, att, att_left,
):
    for w in range(WINS):
        x = window_rows(tok, main, lat, diag, w)
        centred = x - jnp.mean(x, -1, keepdims=True)
        inverse = lax.rsqrt(jnp.mean(centred * centred, -1, keepdims=True) + 1e-05)
        rows = slice(WIN * w, WIN * w + WIN)
        inv_s[rows] = jnp.broadcast_to(inverse, (WIN, 128))
        nrm[rows] = (centred * inverse).astype(BF)
    for i in range(3):
        cols = slice(HD * i, HD * i + HD)
        r = nn(nrm[...], wqkv[:, cols])
        qkv[:, cols] = (r.astype(BF) * FACTOR).astype(BF) if i == 0 else r.astype(BF)

    by_row = jnp.concatenate([land[...].astype(F32), jnp.zeros((12, 104), F32)], 1)
    own_cells = jnp.broadcast_to(by_row[6:12][:, None, :], (6, 2, 128)).reshape(12, 128)
    main_cells, lat_cells, diag_cells = (
        r[r.shape[0] - 1, :, :, 0:128].astype(F32).reshape(12, 128) for r in (main, lat, diag)
    )
    first = lax.broadcasted_iota(jnp.int32, (WIN, SLAB), 1) < HSIZE
    zero = jnp.zeros((WIN, SLAB), BF)
    for w in range(WINS):
        rows = slice(WIN * w, WIN * w + WIN)
        if w < WINS - 1:
            parts = [land_column(own_cells, 3 + 6 * w, 6), land_column(main_cells, 3 + 6 * w, 6)]
            mask = None
        else:
            parts = [
                land_column(c, at, 3)
                for c, at in ((own_cells, 21), (lat_cells, 0), (main_cells, 21), (diag_cells, 0))
            ]
            k_at = lax.broadcasted_iota(jnp.int32, (WIN, WIN), 0) % HALF
            q_at = lax.broadcasted_iota(jnp.int32, (WIN, WIN), 1) % HALF
            apart = (k_at >= HALF // 2) != (q_at >= HALF // 2)
            mask = jnp.where(jnp.logical_and(apart, lax.axis_index("lat") == 1), FAR, 0.0)
        land_key = jnp.broadcast_to(jnp.concatenate(parts, 0), (WIN, WIN))
        for s in range(HEADS // 2):
            q = qkv[rows, SLAB * s : SLAB * s + SLAB]
            k = qkv[rows, HD + SLAB * s : HD + SLAB * s + SLAB]
            v = qkv[rows, 2 * HD + SLAB * s : 2 * HD + SLAB * s + SLAB]
            both = jnp.concatenate([jnp.where(first, k, zero), jnp.where(first, zero, k)], 0)
            sc = nt(both, q).reshape(2, WIN, WIN)
            sc = jnp.stack([sc[e] + land_key * bias[2 * s + e] for e in range(2)])
            if mask is not None:
                sc = sc + mask[None]
            ex = jnp.exp(sc - jnp.max(sc, 1, keepdims=True))
            attn = ex * (1.0 / jnp.sum(ex, 1, keepdims=True))
            attn_s[w, s] = attn
            attn_b = attn.astype(BF)
            o = jnp.where(first, tn(attn_b[0], v), tn(attn_b[1], v))
            att[rows, SLAB * s : SLAB * s + SLAB] = o.astype(BF)
            att_left[w, :, SLAB * s : SLAB * s + SLAB] = o[HALF:].astype(BF)


def backward_kernel(
    cot, main, lat, diag, nrm, qkv, attn_s, att, wout,
    keep, send, dqkv, cotb, datt,
):
    core = lax.axis_index("core")
    for w in range(WINS):
        cotb[WIN * w : WIN * w + WIN] = window_rows(cot, main, lat, diag, w).astype(BF)
    datt[...] = nt(cotb[...], wout[...]).astype(BF)

    first = lax.broadcasted_iota(jnp.int32, (WIN, SLAB), 1) < HSIZE
    zero = jnp.zeros((WIN, SLAB), BF)
    for w in range(WINS):
        rows = slice(WIN * w, WIN * w + WIN)
        for s in range(HEADS // 2):
            q_cols, k_cols, v_cols = (
                slice(HD * i + SLAB * s, HD * i + SLAB * s + SLAB) for i in range(3)
            )
            q, k, v = qkv[rows, q_cols], qkv[rows, k_cols], qkv[rows, v_cols]
            do = datt[rows, q_cols]
            attn = attn_s[w, s]
            both = jnp.concatenate([jnp.where(first, v, zero), jnp.where(first, zero, v)], 0)
            d_attn = nt(both, do).reshape(2, WIN, WIN)
            delta = jnp.sum(attn * d_attn, 1, keepdims=True)
            d_sc = (attn * (d_attn - delta)).astype(BF)
            d_v = nn(attn.astype(BF).reshape(2 * WIN, WIN), do)
            d_k = nn(d_sc.reshape(2 * WIN, WIN), q)
            d_q = jnp.where(first, tn(d_sc[0], k), tn(d_sc[1], k))
            dqkv[rows, q_cols] = (d_q * FACTOR).astype(BF)
            dqkv[rows, k_cols] = jnp.where(first, d_k[:WIN], d_k[WIN:]).astype(BF)
            dqkv[rows, v_cols] = jnp.where(first, d_v[:WIN], d_v[WIN:]).astype(BF)

    def put(r, i, lo):
        wide = r.shape[1]
        r = (r * GRAD_SCALE).reshape(2, 4, 2, 2, 8, wide)
        cols = slice(lo, lo + wide)
        for z in range(2):
            for y in range(4):
                even = r[z, y, :, 0].reshape(16, wide)
                odd = r[z, y, :, 1].reshape(16, wide)
                at = y * 8 + 2 * i + z
                keep[at, :, cols] = jnp.where(core == 0, even, odd)
                send[at, :, cols] = jnp.where(core == 0, odd, even).astype(BF)

    for i in range(4):
        feats = slice(256 * i, 256 * i + 256)
        put(tn(nrm[:, feats], dqkv[...]), i, 0)
        put(tn(cotb[:, feats], att[...]), i, 3 * HD)


def store_rows(r, own, main, lat, w):
    r = r.astype(BF)
    if w < WINS - 1:
        own[3 + 6 * w : 9 + 6 * w, 6:12] = r[:HALF].reshape(6, 6, 2, D)
        main[6 * w : 6 * w + 6] = r[HALF:].reshape(6, 6, 2, D)
    else:
        own[21:24, 6:12] = r[:36].reshape(3, 6, 2, D)
        lat[...] = r[36:72].reshape(3, 6, 2, D)
        main[18:21] = r[72:108].reshape(3, 6, 2, D)
        main[21:24] = r[108:].reshape(3, 6, 2, D)


def out_kernel(att, wout, own, lat):
    for w in range(WINS):
        r = nn(att[WIN * w : WIN * w + 80], wout[...]).astype(BF)
        if w < WINS - 1:
            own[3 + 6 * w : 9 + 6 * w, 6:12] = r[:HALF].reshape(6, 6, 2, D)
        else:
            own[21:24, 6:12] = r[:36].reshape(3, 6, 2, D)
            lat[...] = r[36:72].reshape(3, 6, 2, D)


def home_kernel(att_left, wout, main):
    for w in range(WINS):
        main[6 * w : 6 * w + 6] = nn(att_left[w], wout[...]).astype(BF).reshape(6, 6, 2, D)


def token_kernel(dqkv, wqkv, nrm, inv_s, own, main, lat):
    for w in range(WINS):
        rows = slice(WIN * w, WIN * w + WIN)
        d_normed = nt(dqkv[rows], wqkv[...])
        unit = nrm[rows].astype(F32)
        d_flat = inv_s[rows, 0:1] * (
            d_normed
            - jnp.mean(d_normed, -1, keepdims=True)
            - unit * jnp.mean(d_normed * unit, -1, keepdims=True)
        )
        store_rows(d_flat, own, main, lat, w)


def gray(label):
    return label ^ (label >> 1)


def paired(z):
    return 2 * gray(z >> 1) + (z & 1)


def labels():
    core = lax.axis_index("core")
    y = gray((lax.axis_index("y") + core) & 3)
    return y, paired((lax.axis_index("z") + core) & 7), core


def core_kernel(keep, arrived, kept, s1, s2, s3):
    y_label, z_label, core = labels()
    for (dy, dz), ref in zip(((0, 0),) + PEERS, (kept, s1, s2, s3)):
        y0, z0 = (y_label & 1) ^ dy, (z_label & 1) ^ dz
        for n, (y1, z1, z2) in enumerate(np.ndindex(2, 2, 2)):
            y = (gray(2 * y1 + y0) - core + 4) & 3
            z = (paired(4 * z2 + 2 * z1 + z0) - core + 8) & 7
            at = y * 8 + z
            ref[n] = (keep[at] + arrived[at].astype(F32)).astype(ref.dtype)


def middle_kernel(keep, a1, a2, a3, kept, s1, s2, s3):
    def total(i):
        at = pl.ds(2 * i, 2)
        return keep[at] + a1[at].astype(F32) + a2[at].astype(F32) + a3[at].astype(F32)

    y_label, z_label, _ = labels()
    mine = (y_label >> 1) * 2 + ((z_label >> 1) & 1)
    kept[...] = total(mine)
    for n, ref in enumerate((s1, s2, s3)):
        ref[...] = total(mine ^ (n + 1)).astype(BF)


def late_kernel(keep, a1, a2, a3, kept, send, work):
    work[...] = keep[...] + a1[...].astype(F32) + a2[...].astype(F32) + a3[...].astype(F32)
    _, z_label, _ = labels()
    z = z_label >> 2
    kept[...] = work[z]
    send[...] = work[z ^ 1].astype(BF)


def ring_kernel(keep, arrived, kept, send, work):
    total = keep[...] + arrived[...].astype(F32)
    work[...] = total.reshape(2, 8, 2 * D)
    x = lax.axis_index("xh")
    for ref, at in ((kept, x), (send, x ^ 1)):
        r = work[at]
        ref[...] = jnp.concatenate([r[:, :D], r[:, D:]], 0).astype(BF)


def last_kernel(keep, a1, a2, a3, qkv, out):
    wide = [r[...].astype(F32) for r in (keep, a1, a2, a3)]
    total = (wide[0] + wide[1]) + (wide[2] + wide[3])
    qkv[...] = jnp.concatenate([total[:8], total[8:, :HD]], 1)
    out[...] = total[8:, HD:]


def gather_kernel(out_own, tok_own, o_main, t_main, o_lat, t_lat, out, tok, lat, sems):
    copies = []
    for i, (ref, main, edge) in enumerate(((out, o_main, o_lat), (tok, t_main, t_lat))):
        copies += [
            pltpu.make_async_copy(main.at[0:21], ref.at[3:24, 0:6], sems.at[i, 0]),
            pltpu.make_async_copy(main.at[21:24], lat.at[i, :, 0:6], sems.at[i, 1]),
            pltpu.make_async_copy(edge, lat.at[i, :, 6:12], sems.at[i, 2]),
        ]
    for c in copies:
        c.start()
    for c in copies:
        c.wait()


def finish_kernel(out_part, tok_part, lat, out, tok, sems):
    copies = [
        pltpu.make_async_copy(lat.at[i], ref.at[0:3], sems.at[i])
        for i, ref in enumerate((out, tok))
    ]
    for c in copies:
        c.start()
    for c in copies:
        c.wait()


VM = pl.BlockSpec(memory_space=pltpu.VMEM)
SM = pl.BlockSpec(memory_space=pltpu.SMEM)
ANY = pl.BlockSpec(memory_space=pl.ANY)


def shaped(dims, kind=BF):
    return jax.ShapeDtypeStruct(dims, kind)


def call(body, ins, outs, scratch=(), limit=16, flops=0, name=None, aliases=None, out_spec=VM, moved=8):
    return pl.pallas_call(
        body,
        in_specs=ins,
        out_specs=out_spec if isinstance(out_spec, list) else [out_spec] * len(outs),
        out_shape=outs,
        scratch_shapes=list(scratch),
        input_output_aliases=aliases or {},
        compiler_params=pltpu.CompilerParams(vmem_limit_bytes=limit * 2**20),
        cost_estimate=pl.CostEstimate(flops=0, bytes_accessed=moved * 2**20, transcendentals=0),
        name=name,
    )


def shift(block, axis, step):
    count = lax.axis_size(axis)
    return lax.ppermute(block, axis, [(i, (i + step) % count) for i in range(count)])


def shift_both(block, step):
    count = lax.axis_size(LON)
    route = [
        (i * 2 + b, ((i + step) % count) * 2 + 1 - b) for i in range(count) for b in range(2)
    ]
    return lax.ppermute(block, ALL, route)


def flipped(at, y_bits, z_bits, xh):
    z, y, x, core, lat = at
    y_label = gray((y + core) % 4) ^ y_bits
    y2, z2 = gray(y_label), paired(paired((z + core) % 8) ^ z_bits)
    return ((z2 - core) % 8, (y2 - core) % 4, x ^ xh, core, lat)


def shift_both_x(block):
    return lax.ppermute(block, ("xh", "lat"), [(i, 3 - i) for i in range(4)])


def exchange(block, y_bits, z_bits, xh=0):
    route = []
    for i, at in enumerate(np.ndindex(*SIZES)):
        route.append((i, int(np.ravel_multi_index(flipped(at, y_bits, z_bits, xh), SIZES))))
    return lax.ppermute(block, ALL, route)


def per_device(tokens, land_mask, land_bias, qkv_weight, out_weight, cotangent):
    land = land_mask.T
    full, part, edge = (24, 12, 2, D), (21, 6, 2, D), (3, 6, 2, D)
    dma = pltpu.SemaphoreType.DMA

    main, lat, diag = call(
        tok_halo_kernel,
        [VM, ANY],
        [shaped((22, 6, 2, D)), shaped((4, 6, 2, D)), shaped((4, 6, 2, D))],
        scratch=[
            pltpu.VMEM((22, 6, 2, D), BF),
            pltpu.VMEM((4, 6, 2, D), BF),
            pltpu.VMEM((4, 6, 2, D), BF),
            dma((2, 5)),
        ],
        out_spec=ANY,
        limit=60,
        name="tok_halo",
    )(land, tokens)
    main, qkv_weight, out_weight = lax.optimization_barrier((main, qkv_weight, out_weight))
    main, lat, diag = shift(main, LON, -1), shift(lat, "lat", -1), shift_both(diag, -1)
    wqkv, wout = call(
        weights_kernel,
        [ANY] * 2,
        [shaped((D, 3 * HD)), shaped((HD, D))],
        scratch=[dma((5,))],
        limit=16,
        name="weights",
    )(qkv_weight, out_weight)
    lat, diag, cotangent, wqkv = lax.optimization_barrier((lat, diag, cotangent, wqkv))
    cot_main, cot_lat, cot_diag = call(
        cot_halo_kernel,
        [ANY],
        [shaped(part), shaped(edge), shaped(edge)],
        scratch=[dma((5,))],
        out_spec=ANY,
        limit=16,
        name="cot_halo",
    )(cotangent)
    cot_main = shift(cot_main, LON, -1)
    cot_lat, cot_diag = shift(cot_lat, "lat", -1), shift_both(cot_diag, -1)

    nrm, inverse, qkv, attn, att, att_left = call(
        forward_kernel,
        [SM] + [VM] * 6,
        [
            shaped((TOK, D)),
            shaped((TOK, 128), F32),
            shaped((TOK, 3 * HD)),
            shaped((WINS, HEADS // 2, 2, WIN, WIN), F32),
            shaped((TOK, HD)),
            shaped((WINS, HALF, HD)),
        ],
        limit=16,
        flops=4 * 10**9,
        name="forward",
    )(land_bias, tokens, main, lat, diag, land, wqkv)

    chunks = (32, 16, 2 * D)
    keep, send, dqkv = call(
        backward_kernel,
        [VM] * 9,
        [shaped(chunks, F32), shaped(chunks), shaped((TOK, 3 * HD))],
        scratch=[pltpu.VMEM((TOK, D), BF), pltpu.VMEM((TOK, HD), BF)],
        limit=18,
        flops=4 * 10**9,
        name="backward",
    )(cotangent, cot_main, cot_lat, cot_diag, nrm, qkv, attn, att, wout)

    def summed(body, operands, rows, sent, sends, name, scratch=(), kind=F32, moved=8):
        kept, *rest = call(
            body,
            [VM] * len(operands),
            [shaped(rows, kind)] + [shaped(sent)] * sends,
            scratch=scratch,
            limit=16,
            name=name,
            moved=moved,
        )(*operands)
        return kept, rest

    arrived = shift(send, "core", 1)
    whole = (24, 6, 2, D)
    send, att = lax.optimization_barrier((send, att))
    att_left = shift(att_left, LON, 1)
    out_own, out_lat = call(
        out_kernel,
        [VM] * 2,
        [shaped(full), shaped(edge)],
        limit=16,
        flops=10**9,
        name="out",
    )(att, wout)
    out_lat, keep = lax.optimization_barrier((out_lat, keep))
    eighth, small = (8, 16, 2 * D), (2, 16, 2 * D)
    kept, sends = summed(core_kernel, (keep, arrived), eighth, eighth, 3, "sum_core")
    a = [exchange(s, dy, dz) for (dy, dz), s in zip(PEERS, sends)]
    dqkv, kept, att_left = lax.optimization_barrier((dqkv, kept, att_left))
    tok_own, tok_main, tok_lat = call(
        token_kernel,
        [VM] * 4,
        [shaped(full), shaped(whole), shaped(edge)],
        limit=16,
        flops=2 * 10**9,
        name="token_grad",
    )(dqkv, wqkv, nrm, inverse)
    tok_main = shift(tok_main, LON, 1)
    (out_main,) = call(
        home_kernel, [VM] * 2, [shaped(whole)], limit=16, flops=10**9, name="out_left"
    )(att_left, wout)
    out_main, kept = lax.optimization_barrier((out_main, kept))
    kept, sends = summed(middle_kernel, [kept] + a, small, small, 3, "sum_low")
    a = [exchange(s, 2 * dy, 2 * dz) for (dy, dz), s in zip(PEERS, sends)]
    kept, (s,) = summed(
        late_kernel, [kept] + a, small[1:], small[1:], 1, "sum_next", [pltpu.VMEM(small, F32)]
    )
    out_own, kept = lax.optimization_barrier((out_own, kept))
    block_out, grad_tokens, lat = call(
        gather_kernel,
        [ANY] * 6,
        [shaped(full), shaped(full), shaped((2, 3, 12, 2, D))],
        scratch=[dma((2, 3))],
        aliases={0: 0, 1: 1},
        out_spec=ANY,
        name="gather",
    )(out_own, tok_own, out_main, tok_main, out_lat, tok_lat)
    kept, (s,) = summed(
        ring_kernel,
        (kept, exchange(s, 0, 4)),
        (16, D),
        (16, D),
        1,
        "sum_z",
        [pltpu.VMEM((2, 8, 2 * D), F32)],
        BF,
        64,
    )
    a = [shift(kept, "lat", 1), shift(s, "xh", 1), shift_both_x(s)]
    grad_qkv, grad_out = call(
        last_kernel,
        [VM] * 4,
        [shaped((8, 3 * HD), F32), shaped((8, HD), F32)],
        name="sum_x",
    )(kept, *a)
    block_out, grad_tokens = call(
        finish_kernel,
        [ANY] * 3,
        [shaped(full), shaped(full)],
        scratch=[dma((2,))],
        aliases={0: 0, 1: 1},
        out_spec=ANY,
        name="assemble",
    )(block_out, grad_tokens, shift(lat, "lat", 1))
    return (block_out, grad_tokens, grad_qkv, grad_out.T)


def solution(mesh):
    fine = Mesh(mesh.devices.reshape(SIZES), ALL)
    grid = P("lat", LON, None, None)
    in_specs = (grid, P("lat", LON), P(), P(), P(), grid)
    out_specs = (grid, grid, P(LON, None), P(None, LON))
    return jax.shard_map(
        per_device, mesh=fine, in_specs=in_specs, out_specs=out_specs, check_vma=False
    )
```

profile of v0, /device:TPU:4, one launch (start us, length us, event | category | flops | bytes accessed | tf_op | source)
XLA Modules:
  0.0 93.7 jit_solution(2292013198514663123)
XLA Ops:
  0.6 2.7 %tok_halo.1 = (bf16[22,6,2,1024]{3,2,1,0:T(2,128)(2,1)}, bf16[4,6,2,1024]{3,2,1,0:T(2,128)(2,1)}, bf16[4,6,2,1024]{3,2,1,0:T(2,128)(2,1)}) custom-call(s32[12,24]{1,0:T(8,128)} %bitcast.2, bf16[24,12,2,1024]{3,2,1,0:T(2,128)(2,1)} %tok.3), custom_call_target="tpu_custom_call" | custom-call | bytes 8388608 | tf_op jit(solution)/shard_map/tok_halo/pallas_call | solution.py:403
  3.3 1.3 %collective-permute-start = (bf16[4,6,2,1024]{3,2,1,0:T(2,128)(2,1)}, bf16[4,6,2,1024]{3,2,1,0:T(2,128)(2,1)S(1)}, u32[]{:S(2)}, u32[]{:S(2)}) collective-permute-start(bf16[4,6,2,1024]{3,2,1,0:T(2,128)(2,1)} %get-tuple-element.62), channel_id=1, source_target_pairs={{0,1},{1,0},{2,3},{3,2},{4,5},{5,4},{6,7},{7,6},{8,9},{9,8},{10,11... | collective-permute-start | bytes 294920 | tf_op jit(solution)/shard_map/ppermute | solution.py:369
  4.6 2.8 %collective-permute-start.5 = (bf16[22,6,2,1024]{3,2,1,0:T(2,128)(2,1)}, bf16[22,6,2,1024]{3,2,1,0:T(2,128)(2,1)S(1)}, u32[]{:S(2)}, u32[]{:S(2)}) collective-permute-start(bf16[22,6,2,1024]{3,2,1,0:T(2,128)(2,1)} %get-tuple-element.72), channel_id=1, source_target_pairs={{0,254},{2,0},{4,2},{6,4},{8,6},{10,8},{12,10},{14,12},{16,14},{18... | collective-permute-start | bytes 1622024 | tf_op jit(solution)/shard_map/ppermute | solution.py:369
  7.4 1.9 %copy-done.2 = bf16[1024,1536]{1,0:T(8,128)(2,1)S(1)} copy-done((bf16[1024,1536]{1,0:T(8,128)(2,1)S(1)}, bf16[1024,1536]{1,0:T(8,128)(2,1)}, u32[]{:S(2)}) %copy-start.2) | copy-done | bytes 3145752
  9.3 0.3 weights.1
  9.7 0.0 copy-start.1
  9.7 0.0 copy-start.5
  9.7 0.0 collective-permute-done.lat
  9.7 0.0 collective-permute-done.1.diag
  9.7 0.2 cot_halo.1
  9.9 7.2 %collective-permute-start.2 = (bf16[21,6,2,1024]{3,2,1,0:T(2,128)(2,1)S(1)}, bf16[21,6,2,1024]{3,2,1,0:T(2,128)(2,1)S(1)}, u32[]{:S(2)}, u32[]{:S(2)}) collective-permute-start(bf16[21,6,2,1024]{3,2,1,0:T(2,128)(2,1)S(1)} %get-tuple-element.69), channel_id=1, source_target_pairs={{0,254},{2,0},{4,2},{6,4},{8,6},{10,8},{12,10},{14,12},{16,14},{18... | collective-permute-start | bytes 1548296 | tf_op jit(solution)/shard_map/ppermute | solution.py:369
  17.1 1.2 %collective-permute-start.3 = (bf16[3,6,2,1024]{3,2,1,0:T(2,128)(2,1)S(1)}, bf16[3,6,2,1024]{3,2,1,0:T(2,128)(2,1)S(1)}, u32[]{:S(2)}, u32[]{:S(2)}) collective-permute-start(bf16[3,6,2,1024]{3,2,1,0:T(2,128)(2,1)S(1)} %get-tuple-element.70), channel_id=1, source_target_pairs={{0,1},{1,0},{2,3},{3,2},{4,5},{5,4},{6,7},{7,6},{8,9},{9,8},{10,11... | collective-permute-start | bytes 221192 | tf_op jit(solution)/shard_map/ppermute | solution.py:369
  18.3 1.1 %collective-permute-start.4 = (bf16[3,6,2,1024]{3,2,1,0:T(2,128)(2,1)S(1)}, bf16[3,6,2,1024]{3,2,1,0:T(2,128)(2,1)S(1)}, u32[]{:S(2)}, u32[]{:S(2)}) collective-permute-start(bf16[3,6,2,1024]{3,2,1,0:T(2,128)(2,1)S(1)} %get-tuple-element.71), channel_id=1, source_target_pairs={{0,255},{1,254},{2,1},{3,0},{4,3},{5,2},{6,5},{7,4},{8,7},{9,6},{1... | collective-permute-start | bytes 221192 | tf_op jit(solution)/shard_map/ppermute | solution.py:377
  19.5 6.3 %forward.1 = (bf16[576,1024]{1,0:T(8,128)(2,1)S(1)}, f32[576,128]{1,0:T(8,128)S(1)}, bf16[576,1536]{1,0:T(8,128)(2,1)S(1)}, f32[4,4,2,144,144]{4,3,2,1,0:T(8,128...) custom-call(f32[8]{0:T(128)S(1)} %copy-done.5, bf16[24,12,2,1024]{3,2,1,0:T(2,128)(2,1)S(1)} %copy-done.1, ...), custom_call_target="tpu_custom_call" | custom-call | bytes 8388608 | tf_op jit(solution)/shard_map/forward/pallas_call | solution.py:440
  25.8 1.2 %collective-permute-done.3.lat = bf16[3,6,2,1024]{3,2,1,0:T(2,128)(2,1)S(1)} collective-permute-done((bf16[3,6,2,1024]{3,2,1,0:T(2,128)(2,1)S(1)}, bf16[3,6,2,1024]{3,2,1,0:T(2,128)(2,1)S(1)}, u32[]{:S(2)}, u32[]{:S(2)}) %collective-permute-start.3) | collective-permute-done | bytes 73760 | tf_op jit(solution)/shard_map/ppermute | solution.py:369
  27.0 0.0 collective-permute-done.4.diag
  27.0 0.0 collective-permute-done.2.main
  27.0 8.4 %backward.1 = (f32[32,16,2048]{2,1,0:T(8,128)S(1)}, bf16[32,16,2048]{2,1,0:T(8,128)(2,1)S(1)}, bf16[576,1536]{1,0:T(8,128)(2,1)S(1)}) custom-call(bf16[24,12,2,1024]{3,2,1,0:T(2,128)(2,1)S(1)} %copy-done, bf16[21,6,2,1024]{3,2,1,0:T(2,128)(2,1)S(1)} %collective-permute-done.2.main, bf16[3,6,2,1024]{3,2,1,0:T(2,128)(2,1)S(1)} %collective-permute-done.3.lat, ...), custom_call_target="tpu_custom_call" | custom-call | bytes 8388608 | tf_op jit(solution)/shard_map/backward/pallas_call | solution.py:457
  35.4 0.1 collective-permute-start.6
  35.5 0.5 collective-permute-start.7
  36.0 1.9 %out.1 = (bf16[24,12,2,1024]{3,2,1,0:T(2,128)(2,1)}, bf16[3,6,2,1024]{3,2,1,0:T(2,128)(2,1)S(1)}) custom-call(bf16[576,512]{1,0:T(8,128)(2,1)S(1)} %get-tuple-element.82.att, bf16[512,1024]{1,0:T(8,128)(2,1)S(1)} %get-tuple-element.80.wout), custom_call_target="tpu_custom_call" | custom-call | bytes 8388608 | tf_op jit(solution)/shard_map/out/pallas_call | solution.py:483
  37.9 1.8 %collective-permute-done.6.arrived = bf16[32,16,2048]{2,1,0:T(8,128)(2,1)S(1)} collective-permute-done((bf16[32,16,2048]{2,1,0:T(8,128)(2,1)S(1)}, bf16[32,16,2048]{2,1,0:T(8,128)(2,1)S(1)}, u32[]{:S(2)}, u32[]{:S(2)}) %collective-permute-start.6) | collective-permute-done | bytes 2097184 | tf_op jit(solution)/shard_map/ppermute | solution.py:369
  39.7 0.3 sum_core.1
  40.0 0.1 collective-permute-start.8
  40.1 1.0 %collective-permute-start.9 = (bf16[8,16,2048]{2,1,0:T(8,128)(2,1)S(1)}, bf16[8,16,2048]{2,1,0:T(8,128)(2,1)S(1)}, u32[]{:S(2)}, u32[]{:S(2)}) collective-permute-start(bf16[8,16,2048]{2,1,0:T(8,128)(2,1)S(1)} %get-tuple-element.94), channel_id=1, source_target_pairs={{0,8},{1,9},{2,26},{3,27},{4,12},{5,13},{6,30},{7,31},{8,0},{9,1},... | collective-permute-start | bytes 1572872 | tf_op jit(solution)/shard_map/ppermute | solution.py:395
  41.1 2.5 %collective-permute-start.10 = (bf16[8,16,2048]{2,1,0:T(8,128)(2,1)S(1)}, bf16[8,16,2048]{2,1,0:T(8,128)(2,1)S(1)}, u32[]{:S(2)}, u32[]{:S(2)}) collective-permute-start(bf16[8,16,2048]{2,1,0:T(8,128)(2,1)S(1)} %get-tuple-element.95), channel_id=1, source_target_pairs={{0,40},{1,41},{2,250},{3,251},{4,44},{5,45},{6,254},{7,255},{8,32}... | collective-permute-start | bytes 1572872 | tf_op jit(solution)/shard_map/ppermute | solution.py:395
  43.6 1.3 %collective-permute-done.7.att_left = bf16[4,72,512]{2,1,0:T(8,128)(2,1)S(1)} collective-permute-done((bf16[4,72,512]{2,1,0:T(8,128)(2,1)S(1)}, bf16[4,72,512]{2,1,0:T(8,128)(2,1)S(1)}, u32[]{:S(2)}, u32[]{:S(2)}) %collective-permute-start.7) | collective-permute-done | bytes 294944 | tf_op jit(solution)/shard_map/ppermute | solution.py:369
  44.9 5.4 %token_grad.1 = (bf16[24,12,2,1024]{3,2,1,0:T(2,128)(2,1)}, bf16[24,6,2,1024]{3,2,1,0:T(2,128)(2,1)S(1)}, bf16[3,6,2,1024]{3,2,1,0:T(2,128)(2,1)S(1)}) custom-call(bf16[576,1536]{1,0:T(8,128)(2,1)S(1)} %get-tuple-element.102.dqkv, bf16[1024,1536]{1,0:T(8,128)(2,1)S(1)} %get-tuple-element.75.wqkv, bf16[576,1024]{1,0:T(8,128)(2,1)S(1)} %get-tuple-element.76.nrm, ...), custom_call_target="tpu_custom_call" | custom-call | bytes 8388608 | tf_op jit(solution)/shard_map/token_grad/pallas_call | solution.py:496
  50.3 4.6 %collective-permute-start.14 = (bf16[24,6,2,1024]{3,2,1,0:T(2,128)(2,1)S(1)}, bf16[24,6,2,1024]{3,2,1,0:T(2,128)(2,1)S(1)}, u32[]{:S(2)}, u32[]{:S(2)}) collective-permute-start(bf16[24,6,2,1024]{3,2,1,0:T(2,128)(2,1)S(1)} %get-tuple-element.106), channel_id=1, source_target_pairs={{0,2},{2,4},{4,6},{6,8},{8,10},{10,12},{12,14},{14,16},{16,18},{18... | collective-permute-start | bytes 1769480 | tf_op jit(solution)/shard_map/ppermute | solution.py:369
  54.9 0.9 out_left.1.o_main
  55.8 0.0 collective-permute-done.9.a2
  55.8 0.3 sum_low.1
  56.0 1.9 %collective-permute-start.11 = (bf16[2,16,2048]{2,1,0:T(8,128)(2,1)S(1)}, bf16[2,16,2048]{2,1,0:T(8,128)(2,1)S(1)}, u32[]{:S(2)}, u32[]{:S(2)}) collective-permute-start(bf16[2,16,2048]{2,1,0:T(8,128)(2,1)S(1)} %get-tuple-element.97), channel_id=1, source_target_pairs={{0,64},{1,65},{2,66},{3,67},{4,68},{5,69},{6,70},{7,71},{8,72},{9,... | collective-permute-start | bytes 393224 | tf_op jit(solution)/shard_map/ppermute | solution.py:395
  57.9 6.2 %collective-permute-start.12 = (bf16[2,16,2048]{2,1,0:T(8,128)(2,1)S(1)}, bf16[2,16,2048]{2,1,0:T(8,128)(2,1)S(1)}, u32[]{:S(2)}, u32[]{:S(2)}) collective-permute-start(bf16[2,16,2048]{2,1,0:T(8,128)(2,1)S(1)} %get-tuple-element.98), channel_id=1, source_target_pairs={{0,24},{1,25},{2,10},{3,11},{4,28},{5,29},{6,14},{7,15},{8,16},{9,... | collective-permute-start | bytes 393224 | tf_op jit(solution)/shard_map/ppermute | solution.py:395
  64.2 2.9 %collective-permute-done.12.a2 = bf16[2,16,2048]{2,1,0:T(8,128)(2,1)S(1)} collective-permute-done((bf16[2,16,2048]{2,1,0:T(8,128)(2,1)S(1)}, bf16[2,16,2048]{2,1,0:T(8,128)(2,1)S(1)}, u32[]{:S(2)}, u32[]{:S(2)}) %collective-permute-start.12) | collective-permute-done | bytes 131104 | tf_op jit(solution)/shard_map/ppermute | solution.py:395
  67.1 6.7 %collective-permute-done.13.a3 = bf16[2,16,2048]{2,1,0:T(8,128)(2,1)S(1)} collective-permute-done((bf16[2,16,2048]{2,1,0:T(8,128)(2,1)S(1)}, bf16[2,16,2048]{2,1,0:T(8,128)(2,1)S(1)}, u32[]{:S(2)}, u32[]{:S(2)}) %collective-permute-start.13) | collective-permute-done | bytes 131104 | tf_op jit(solution)/shard_map/ppermute | solution.py:395
  73.8 0.1 sum_next.1
  73.9 1.0 %gather.1 = (bf16[24,12,2,1024]{3,2,1,0:T(2,128)(2,1)}, bf16[24,12,2,1024]{3,2,1,0:T(2,128)(2,1)}, bf16[2,3,12,2,1024]{4,3,2,1,0:T(2,128)(2,1)S(1)}) custom-call(bf16[24,12,2,1024]{3,2,1,0:T(2,128)(2,1)} %get-tuple-element.101.out_own, bf16[24,12,2,1024]{3,2,1,0:T(2,128)(2,1)} %get-tuple-element.104.tok_own, ...), custom_call_target="tpu_custom_call", output_to_operand_aliasing={{0}: (0, {}), {1}: (1, {})} | custom-call | bytes 8388608 | tf_op jit(solution)/shard_map/gather/pallas_call | solution.py:515
  74.9 2.3 %collective-permute-start.15 = (bf16[2,3,12,2,1024]{4,3,2,1,0:T(2,128)(2,1)S(1)}, bf16[2,3,12,2,1024]{4,3,2,1,0:T(2,128)(2,1)S(1)}, u32[]{:S(2)}, u32[]{:S(2)}) collective-permute-start(bf16[2,3,12,2,1024]{4,3,2,1,0:T(2,128)(2,1)S(1)} %get-tuple-element.111), channel_id=1, source_target_pairs={{0,1},{1,0},{2,3},{3,2},{4,5},{5,4},{6,7},{7,6},{8,9},{9,8},{10,11... | collective-permute-start | bytes 884744 | tf_op jit(solution)/shard_map/ppermute | solution.py:369
  77.2 4.8 %collective-permute-start.16 = (bf16[16,2048]{1,0:T(8,128)(2,1)S(1)}, bf16[16,2048]{1,0:T(8,128)(2,1)S(1)}, u32[]{:S(2)}, u32[]{:S(2)}) collective-permute-start(bf16[16,2048]{1,0:T(8,128)(2,1)S(1)} %get-tuple-element.115), channel_id=1, source_target_pairs={{0,192},{1,193},{2,194},{3,195},{4,196},{5,197},{6,198},{7,199},{8... | collective-permute-start | bytes 196616 | tf_op jit(solution)/shard_map/ppermute | solution.py:395
  82.0 2.2 %collective-permute-done.16.arrived = bf16[16,2048]{1,0:T(8,128)(2,1)S(1)} collective-permute-done((bf16[16,2048]{1,0:T(8,128)(2,1)S(1)}, bf16[16,2048]{1,0:T(8,128)(2,1)S(1)}, u32[]{:S(2)}, u32[]{:S(2)}) %collective-permute-start.16) | collective-permute-done | bytes 65568 | tf_op jit(solution)/shard_map/ppermute | solution.py:395
  84.2 0.2 collective-permute-start.17
  84.4 2.3 %collective-permute-start.19 = (bf16[16,1024]{1,0:T(8,128)(2,1)S(1)}, bf16[16,1024]{1,0:T(8,128)(2,1)S(1)}, u32[]{:S(2)}, u32[]{:S(2)}) collective-permute-start(bf16[16,1024]{1,0:T(8,128)(2,1)S(1)} %get-tuple-element.117), channel_id=1, source_target_pairs={{0,5},{1,4},{4,1},{5,0},{2,7},{3,6},{6,3},{7,2},{8,13},{9,12},{12,... | collective-permute-start | bytes 98312 | tf_op jit(solution)/shard_map/ppermute | solution.py:388
  86.8 1.7 %collective-permute-start.18 = (bf16[16,1024]{1,0:T(8,128)(2,1)S(1)}, bf16[16,1024]{1,0:T(8,128)(2,1)S(1)}, u32[]{:S(2)}, u32[]{:S(2)}) collective-permute-start(bf16[16,1024]{1,0:T(8,128)(2,1)S(1)} %get-tuple-element.117), channel_id=1, source_target_pairs={{0,4},{4,0},{1,5},{5,1},{2,6},{6,2},{3,7},{7,3},{8,12},{12,8},{9,1... | collective-permute-start | bytes 98312 | tf_op jit(solution)/shard_map/ppermute | solution.py:369
  88.4 0.2 collective-permute-done.19.a3
  88.7 3.5 %collective-permute-done.18.a2 = bf16[16,1024]{1,0:T(8,128)(2,1)S(1)} collective-permute-done((bf16[16,1024]{1,0:T(8,128)(2,1)S(1)}, bf16[16,1024]{1,0:T(8,128)(2,1)S(1)}, u32[]{:S(2)}, u32[]{:S(2)}) %collective-permute-start.18) | collective-permute-done | bytes 32800 | tf_op jit(solution)/shard_map/ppermute | solution.py:369
  92.2 0.6 sum_x.1
  92.8 0.7 assemble.1
  (19 shorter events, 0.1 us)
Async XLA Ops:
  0.6 6.8 %copy-start.3 = (bf16[512,1024]{1,0:T(8,128)(2,1)S(1)}, bf16[512,1024]{1,0:T(8,128)(2,1)}, u32[]{:S(2)}) copy-start(bf16[512,1024]{1,0:T(8,128)(2,1)} %wout_hbm) | copy-start | bytes 3145732
  3.3 6.3 %collective-permute-start = (bf16[4,6,2,1024]{3,2,1,0:T(2,128)(2,1)}, bf16[4,6,2,1024]{3,2,1,0:T(2,128)(2,1)S(1)}, u32[]{:S(2)}, u32[]{:S(2)}) collective-permute-start(bf16[4,6,2,1024]{3,2,1,0:T(2,128)(2,1)} %get-tuple-element.62), channel_id=1, source_target_pairs={{0,1},{1,0},{2,3},{3,2},{4,5},{5,4},{6,7},{7,6},{8,9},{9,8},{10,11... | collective-permute-start | bytes 294920 | tf_op jit(solution)/shard_map/ppermute | solution.py:369
  4.6 5.1 %collective-permute-start.1 = (bf16[4,6,2,1024]{3,2,1,0:T(2,128)(2,1)}, bf16[4,6,2,1024]{3,2,1,0:T(2,128)(2,1)S(1)}, u32[]{:S(2)}, u32[]{:S(2)}) collective-permute-start(bf16[4,6,2,1024]{3,2,1,0:T(2,128)(2,1)} %get-tuple-element.63), channel_id=1, source_target_pairs={{0,255},{1,254},{2,1},{3,0},{4,3},{5,2},{6,5},{7,4},{8,7},{9,6},{1... | collective-permute-start | bytes 294920 | tf_op jit(solution)/shard_map/ppermute | solution.py:377
  4.6 5.1 %copy-start = (bf16[24,12,2,1024]{3,2,1,0:T(2,128)(2,1)S(1)}, bf16[24,12,2,1024]{3,2,1,0:T(2,128)(2,1)}, u32[]{:S(2)}) copy-start(bf16[24,12,2,1024]{3,2,1,0:T(2,128)(2,1)} %cot.1) | copy-start | bytes 3538948
  4.6 14.8 %collective-permute-start.5 = (bf16[22,6,2,1024]{3,2,1,0:T(2,128)(2,1)}, bf16[22,6,2,1024]{3,2,1,0:T(2,128)(2,1)S(1)}, u32[]{:S(2)}, u32[]{:S(2)}) collective-permute-start(bf16[22,6,2,1024]{3,2,1,0:T(2,128)(2,1)} %get-tuple-element.72), channel_id=1, source_target_pairs={{0,254},{2,0},{4,2},{6,4},{8,6},{10,8},{12,10},{14,12},{16,14},{18... | collective-permute-start | bytes 1622024 | tf_op jit(solution)/shard_map/ppermute | solution.py:369
  7.4 1.9 %copy-start.2 = (bf16[1024,1536]{1,0:T(8,128)(2,1)S(1)}, bf16[1024,1536]{1,0:T(8,128)(2,1)}, u32[]{:S(2)}) copy-start(bf16[1024,1536]{1,0:T(8,128)(2,1)} %wqkv_hbm) | copy-start | bytes 9437188
  9.3 10.1 %copy-start.4 = (s32[24,12]{0,1:T(8,128)S(1)}, s32[24,12]{0,1:T(8,128)}, u32[]{:S(2)}) copy-start(s32[24,12]{0,1:T(8,128)} %param.7) | copy-start | bytes 3460
  9.7 9.8 %copy-start.1 = (bf16[24,12,2,1024]{3,2,1,0:T(2,128)(2,1)S(1)}, bf16[24,12,2,1024]{3,2,1,0:T(2,128)(2,1)}, u32[]{:S(2)}) copy-start(bf16[24,12,2,1024]{3,2,1,0:T(2,128)(2,1)} %tok.3) | copy-start | bytes 3538948
  9.7 9.8 %copy-start.5 = (f32[8]{0:T(128)S(1)}, f32[8]{0:T(128)}, u32[]{:S(2)}) copy-start(f32[8]{0:T(128)} %bias.1) | copy-start | bytes 100
  9.9 17.1 %collective-permute-start.2 = (bf16[21,6,2,1024]{3,2,1,0:T(2,128)(2,1)S(1)}, bf16[21,6,2,1024]{3,2,1,0:T(2,128)(2,1)S(1)}, u32[]{:S(2)}, u32[]{:S(2)}) collective-permute-start(bf16[21,6,2,1024]{3,2,1,0:T(2,128)(2,1)S(1)} %get-tuple-element.69), channel_id=1, source_target_pairs={{0,254},{2,0},{4,2},{6,4},{8,6},{10,8},{12,10},{14,12},{16,14},{18... | collective-permute-start | bytes 1548296 | tf_op jit(solution)/shard_map/ppermute | solution.py:369
  17.1 9.9 %collective-permute-start.3 = (bf16[3,6,2,1024]{3,2,1,0:T(2,128)(2,1)S(1)}, bf16[3,6,2,1024]{3,2,1,0:T(2,128)(2,1)S(1)}, u32[]{:S(2)}, u32[]{:S(2)}) collective-permute-start(bf16[3,6,2,1024]{3,2,1,0:T(2,128)(2,1)S(1)} %get-tuple-element.70), channel_id=1, source_target_pairs={{0,1},{1,0},{2,3},{3,2},{4,5},{5,4},{6,7},{7,6},{8,9},{9,8},{10,11... | collective-permute-start | bytes 221192 | tf_op jit(solution)/shard_map/ppermute | solution.py:369
  18.3 8.7 %collective-permute-start.4 = (bf16[3,6,2,1024]{3,2,1,0:T(2,128)(2,1)S(1)}, bf16[3,6,2,1024]{3,2,1,0:T(2,128)(2,1)S(1)}, u32[]{:S(2)}, u32[]{:S(2)}) collective-permute-start(bf16[3,6,2,1024]{3,2,1,0:T(2,128)(2,1)S(1)} %get-tuple-element.71), channel_id=1, source_target_pairs={{0,255},{1,254},{2,1},{3,0},{4,3},{5,2},{6,5},{7,4},{8,7},{9,6},{1... | collective-permute-start | bytes 221192 | tf_op jit(solution)/shard_map/ppermute | solution.py:377
  35.4 4.2 %collective-permute-start.6 = (bf16[32,16,2048]{2,1,0:T(8,128)(2,1)S(1)}, bf16[32,16,2048]{2,1,0:T(8,128)(2,1)S(1)}, u32[]{:S(2)}, u32[]{:S(2)}) collective-permute-start(bf16[32,16,2048]{2,1,0:T(8,128)(2,1)S(1)} %get-tuple-element.81), channel_id=1, source_target_pairs={{0,2},{2,0},{1,3},{3,1},{4,6},{6,4},{5,7},{7,5},{8,10},{10,8},{9,1... | collective-permute-start | bytes 6291464 | tf_op jit(solution)/shard_map/ppermute | solution.py:369
  35.5 9.4 %collective-permute-start.7 = (bf16[4,72,512]{2,1,0:T(8,128)(2,1)S(1)}, bf16[4,72,512]{2,1,0:T(8,128)(2,1)S(1)}, u32[]{:S(2)}, u32[]{:S(2)}) collective-permute-start(bf16[4,72,512]{2,1,0:T(8,128)(2,1)S(1)} %get-tuple-element.89), channel_id=1, source_target_pairs={{0,2},{2,4},{4,6},{6,8},{8,10},{10,12},{12,14},{14,16},{16,18},{18... | collective-permute-start | bytes 884744 | tf_op jit(solution)/shard_map/ppermute | solution.py:369
  40.0 15.7 %collective-permute-start.8 = (bf16[8,16,2048]{2,1,0:T(8,128)(2,1)S(1)}, bf16[8,16,2048]{2,1,0:T(8,128)(2,1)S(1)}, u32[]{:S(2)}, u32[]{:S(2)}) collective-permute-start(bf16[8,16,2048]{2,1,0:T(8,128)(2,1)S(1)} %get-tuple-element.93), channel_id=1, source_target_pairs={{0,32},{1,33},{2,226},{3,227},{4,36},{5,37},{6,230},{7,231},{8,40}... | collective-permute-start | bytes 1572872 | tf_op jit(solution)/shard_map/ppermute | solution.py:395
  40.1 15.6 %collective-permute-start.9 = (bf16[8,16,2048]{2,1,0:T(8,128)(2,1)S(1)}, bf16[8,16,2048]{2,1,0:T(8,128)(2,1)S(1)}, u32[]{:S(2)}, u32[]{:S(2)}) collective-permute-start(bf16[8,16,2048]{2,1,0:T(8,128)(2,1)S(1)} %get-tuple-element.94), channel_id=1, source_target_pairs={{0,8},{1,9},{2,26},{3,27},{4,12},{5,13},{6,30},{7,31},{8,0},{9,1},... | collective-permute-start | bytes 1572872 | tf_op jit(solution)/shard_map/ppermute | solution.py:395
  41.1 14.7 %collective-permute-start.10 = (bf16[8,16,2048]{2,1,0:T(8,128)(2,1)S(1)}, bf16[8,16,2048]{2,1,0:T(8,128)(2,1)S(1)}, u32[]{:S(2)}, u32[]{:S(2)}) collective-permute-start(bf16[8,16,2048]{2,1,0:T(8,128)(2,1)S(1)} %get-tuple-element.95), channel_id=1, source_target_pairs={{0,40},{1,41},{2,250},{3,251},{4,44},{5,45},{6,254},{7,255},{8,32}... | collective-permute-start | bytes 1572872 | tf_op jit(solution)/shard_map/ppermute | solution.py:395
  50.3 23.6 %collective-permute-start.14 = (bf16[24,6,2,1024]{3,2,1,0:T(2,128)(2,1)S(1)}, bf16[24,6,2,1024]{3,2,1,0:T(2,128)(2,1)S(1)}, u32[]{:S(2)}, u32[]{:S(2)}) collective-permute-start(bf16[24,6,2,1024]{3,2,1,0:T(2,128)(2,1)S(1)} %get-tuple-element.106), channel_id=1, source_target_pairs={{0,2},{2,4},{4,6},{6,8},{8,10},{10,12},{12,14},{14,16},{16,18},{18... | collective-permute-start | bytes 1769480 | tf_op jit(solution)/shard_map/ppermute | solution.py:369
  56.0 8.1 %collective-permute-start.11 = (bf16[2,16,2048]{2,1,0:T(8,128)(2,1)S(1)}, bf16[2,16,2048]{2,1,0:T(8,128)(2,1)S(1)}, u32[]{:S(2)}, u32[]{:S(2)}) collective-permute-start(bf16[2,16,2048]{2,1,0:T(8,128)(2,1)S(1)} %get-tuple-element.97), channel_id=1, source_target_pairs={{0,64},{1,65},{2,66},{3,67},{4,68},{5,69},{6,70},{7,71},{8,72},{9,... | collective-permute-start | bytes 393224 | tf_op jit(solution)/shard_map/ppermute | solution.py:395
  57.9 9.2 %collective-permute-start.12 = (bf16[2,16,2048]{2,1,0:T(8,128)(2,1)S(1)}, bf16[2,16,2048]{2,1,0:T(8,128)(2,1)S(1)}, u32[]{:S(2)}, u32[]{:S(2)}) collective-permute-start(bf16[2,16,2048]{2,1,0:T(8,128)(2,1)S(1)} %get-tuple-element.98), channel_id=1, source_target_pairs={{0,24},{1,25},{2,10},{3,11},{4,28},{5,29},{6,14},{7,15},{8,16},{9,... | collective-permute-start | bytes 393224 | tf_op jit(solution)/shard_map/ppermute | solution.py:395
  64.2 9.6 %collective-permute-start.13 = (bf16[2,16,2048]{2,1,0:T(8,128)(2,1)S(1)}, bf16[2,16,2048]{2,1,0:T(8,128)(2,1)S(1)}, u32[]{:S(2)}, u32[]{:S(2)}) collective-permute-start(bf16[2,16,2048]{2,1,0:T(8,128)(2,1)S(1)} %get-tuple-element.99), channel_id=1, source_target_pairs={{0,88},{1,89},{2,74},{3,75},{4,92},{5,93},{6,78},{7,79},{8,80},{9,... | collective-permute-start | bytes 393224 | tf_op jit(solution)/shard_map/ppermute | solution.py:395
  74.9 17.9 %collective-permute-start.15 = (bf16[2,3,12,2,1024]{4,3,2,1,0:T(2,128)(2,1)S(1)}, bf16[2,3,12,2,1024]{4,3,2,1,0:T(2,128)(2,1)S(1)}, u32[]{:S(2)}, u32[]{:S(2)}) collective-permute-start(bf16[2,3,12,2,1024]{4,3,2,1,0:T(2,128)(2,1)S(1)} %get-tuple-element.111), channel_id=1, source_target_pairs={{0,1},{1,0},{2,3},{3,2},{4,5},{5,4},{6,7},{7,6},{8,9},{9,8},{10,11... | collective-permute-start | bytes 884744 | tf_op jit(solution)/shard_map/ppermute | solution.py:369
  77.2 7.0 %collective-permute-start.16 = (bf16[16,2048]{1,0:T(8,128)(2,1)S(1)}, bf16[16,2048]{1,0:T(8,128)(2,1)S(1)}, u32[]{:S(2)}, u32[]{:S(2)}) collective-permute-start(bf16[16,2048]{1,0:T(8,128)(2,1)S(1)} %get-tuple-element.115), channel_id=1, source_target_pairs={{0,192},{1,193},{2,194},{3,195},{4,196},{5,197},{6,198},{7,199},{8... | collective-permute-start | bytes 196616 | tf_op jit(solution)/shard_map/ppermute | solution.py:395
  84.2 4.2 %collective-permute-start.17 = (bf16[16,1024]{1,0:T(8,128)(2,1)S(1)}, bf16[16,1024]{1,0:T(8,128)(2,1)S(1)}, u32[]{:S(2)}, u32[]{:S(2)}) collective-permute-start(bf16[16,1024]{1,0:T(8,128)(2,1)S(1)} %get-tuple-element.116.keep), channel_id=1, source_target_pairs={{0,1},{1,0},{2,3},{3,2},{4,5},{5,4},{6,7},{7,6},{8,9},{9,8},{10,11... | collective-permute-start | bytes 98312 | tf_op jit(solution)/shard_map/ppermute | solution.py:369
  84.4 4.2 %collective-permute-start.19 = (bf16[16,1024]{1,0:T(8,128)(2,1)S(1)}, bf16[16,1024]{1,0:T(8,128)(2,1)S(1)}, u32[]{:S(2)}, u32[]{:S(2)}) collective-permute-start(bf16[16,1024]{1,0:T(8,128)(2,1)S(1)} %get-tuple-element.117), channel_id=1, source_target_pairs={{0,5},{1,4},{4,1},{5,0},{2,7},{3,6},{6,3},{7,2},{8,13},{9,12},{12,... | collective-permute-start | bytes 98312 | tf_op jit(solution)/shard_map/ppermute | solution.py:388
  86.8 5.4 %collective-permute-start.18 = (bf16[16,1024]{1,0:T(8,128)(2,1)S(1)}, bf16[16,1024]{1,0:T(8,128)(2,1)S(1)}, u32[]{:S(2)}, u32[]{:S(2)}) collective-permute-start(bf16[16,1024]{1,0:T(8,128)(2,1)S(1)} %get-tuple-element.117), channel_id=1, source_target_pairs={{0,4},{4,0},{1,5},{5,1},{2,6},{6,2},{3,7},{7,3},{8,12},{12,8},{9,1... | collective-permute-start | bytes 98312 | tf_op jit(solution)/shard_map/ppermute | solution.py:369
where the time goes:
time: 93.9 us; the launch traced here: 93.7 us
  starting transfers between devices  41.6 us (44%)
  Pallas kernels  29.2 us (31%)
  waiting for transfers between devices  20 us (21%)
  local copies, waits for them, and re-layouts  1.91 us (2%)
  between operations  1 us (1%)
    ppermute x10, starting transfers between devices, shift(): lax.ppermute(block, axis, [(i, (i + step) % count) for i in range(count)])  21.8 us
    ppermute x7, starting transfers between devices, exchange(): return lax.ppermute(block, ALL, route)  16.4 us
    ppermute x7, waiting for transfers between devices, exchange(): return lax.ppermute(block, ALL, route)  11.9 us
    pallas_call x1, Pallas kernels, per_device(): call(backward_kernel, [VM] * 9, [shaped(chunks, F32), shaped(chunks), sha...  8.42 us
    ppermute x10, waiting for transfers between devices, shift(): lax.ppermute(block, axis, [(i, (i + step) % count) for i in range(count)])  7.91 us
    pallas_call x1, Pallas kernels, per_device(): call(forward_kernel, [SM] + [VM] * 6, [shaped((TOK, D)), shaped((TOK, 128...  6.29 us
    pallas_call x1, Pallas kernels, per_device(): call(token_kernel, [VM] * 4, [shaped(full), shaped(whole), shaped(edge)],...  5.39 us
    pallas_call x1, Pallas kernels, per_device(): call(tok_halo_kernel, [VM, ANY], [shaped((22, 6, 2, D)), shaped((4, 6, 2,...  2.69 us
  transfers between devices with their start and end apart: 20, of which 8 were waited for; matrix products, arithmetic and copies ran while one was open for 0% of the time, Pallas kernels for 17%

commit v1 on v0

--- a/solution.py
+++ b/solution.py
@@ -199,7 +199,7 @@
 
     def put(r, i, lo):
         wide = r.shape[1]
-        r = (r * GRAD_SCALE).reshape(2, 4, 2, 2, 8, wide)
+        r = r.reshape(2, 4, 2, 2, 8, wide)
         cols = slice(lo, lo + wide)
         for z in range(2):
             for y in range(4):
@@ -311,30 +311,31 @@
 
 def last_kernel(keep, a1, a2, a3, qkv, out):
     wide = [r[...].astype(F32) for r in (keep, a1, a2, a3)]
-    total = (wide[0] + wide[1]) + (wide[2] + wide[3])
+    total = ((wide[0] + wide[1]) + (wide[2] + wide[3])) * GRAD_SCALE
     qkv[...] = jnp.concatenate([total[:8], total[8:, :HD]], 1)
     out[...] = total[8:, HD:]
 
 
-def gather_kernel(out_own, tok_own, o_main, t_main, o_lat, t_lat, out, tok, lat, sems):
+def gather_kernel(o_main, t_main, o_lat, t_lat, lat, sems):
     copies = []
-    for i, (ref, main, edge) in enumerate(((out, o_main, o_lat), (tok, t_main, t_lat))):
+    for i, (main, edge) in enumerate(((o_main, o_lat), (t_main, t_lat))):
+        copies += [
+            pltpu.make_async_copy(main.at[21:24], lat.at[i, :, 0:6], sems.at[i, 0]),
+            pltpu.make_async_copy(edge, lat.at[i, :, 6:12], sems.at[i, 1]),
+        ]
+    for c in copies:
+        c.start()
+    for c in copies:
+        c.wait()
+
+
+def finish_kernel(out_own, tok_own, o_main, t_main, lat, out, tok, sems):
+    copies = []
+    for i, (ref, main) in enumerate(((out, o_main), (tok, t_main))):
         copies += [
             pltpu.make_async_copy(main.at[0:21], ref.at[3:24, 0:6], sems.at[i, 0]),
-            pltpu.make_async_copy(main.at[21:24], lat.at[i, :, 0:6], sems.at[i, 1]),
-            pltpu.make_async_copy(edge, lat.at[i, :, 6:12], sems.at[i, 2]),
+            pltpu.make_async_copy(lat.at[i], ref.at[0:3], sems.at[i, 1]),
         ]
-    for c in copies:
-        c.start()
-    for c in copies:
-        c.wait()
-
-
-def finish_kernel(out_part, tok_part, lat, out, tok, sems):
-    copies = [
-        pltpu.make_async_copy(lat.at[i], ref.at[0:3], sems.at[i])
-        for i, ref in enumerate((out, tok))
-    ]
     for c in copies:
         c.start()
     for c in copies:
@@ -511,16 +512,15 @@
     kept, (s,) = summed(
         late_kernel, [kept] + a, small[1:], small[1:], 1, "sum_next", [pltpu.VMEM(small, F32)]
     )
-    out_own, kept = lax.optimization_barrier((out_own, kept))
-    block_out, grad_tokens, lat = call(
+    out_main, kept = lax.optimization_barrier((out_main, kept))
+    (lat,) = call(
         gather_kernel,
-        [ANY] * 6,
-        [shaped(full), shaped(full), shaped((2, 3, 12, 2, D))],
-        scratch=[dma((2, 3))],
-        aliases={0: 0, 1: 1},
+        [ANY] * 4,
+        [shaped((2, 3, 12, 2, D))],
+        scratch=[dma((2, 2))],
         out_spec=ANY,
         name="gather",
-    )(out_own, tok_own, out_main, tok_main, out_lat, tok_lat)
+    )(out_main, tok_main, out_lat, tok_lat)
     kept, (s,) = summed(
         ring_kernel,
         (kept, exchange(s, 0, 4)),
@@ -533,21 +533,22 @@
         64,
     )
     a = [shift(kept, "lat", 1), shift(s, "xh", 1), shift_both_x(s)]
+    block_out, grad_tokens = call(
+        finish_kernel,
+        [ANY] * 5,
+        [shaped(full), shaped(full)],
+        scratch=[dma((2, 2))],
+        aliases={0: 0, 1: 1},
+        out_spec=ANY,
+        name="assemble",
+    )(out_own, tok_own, out_main, tok_main, shift(lat, "lat", 1))
+    block_out, kept = lax.optimization_barrier((block_out, kept))
     grad_qkv, grad_out = call(
         last_kernel,
         [VM] * 4,
         [shaped((8, 3 * HD), F32), shaped((8, HD), F32)],
         name="sum_x",
     )(kept, *a)
-    block_out, grad_tokens = call(
-        finish_kernel,
-        [ANY] * 3,
-        [shaped(full), shaped(full)],
-        scratch=[dma((2,))],
-        aliases={0: 0, 1: 1},
-        out_spec=ANY,
-        name="assemble",
-    )(block_out, grad_tokens, shift(lat, "lat", 1))
     return (block_out, grad_tokens, grad_qkv, grad_out.T)
 
 

time: 93.9 us -> 92.1 us (0.981)
  waiting for transfers between devices: 20 us -> 18.8 us
    ppermute x10, waiting for transfers between devices: 7.91 us -> 6.94 us  [shift(): lax.ppermute(block, axis, [(i, (i + step) % count) for i in range(count)])]
  transfers between devices with their start and end apart: 20 -> 20, of which waited for: 8 -> 7; matrix products, arithmetic and copies ran while one was open for 0% -> 0% of each run, Pallas kernels for 17% -> 18%
where the time goes in v1:
time: 92.1 us; the launch traced here: 92 us
  starting transfers between devices  41.7 us (45%)
  Pallas kernels  28.7 us (31%)
  waiting for transfers between devices  18.8 us (20%)
  local copies, waits for them, and re-layouts  1.91 us (2%)
    ppermute x10, starting transfers between devices, shift(): lax.ppermute(block, axis, [(i, (i + step) % count) for i in range(count)])  21.9 us
    ppermute x7, starting transfers between devices, exchange(): return lax.ppermute(block, ALL, route)  16.5 us
    ppermute x7, waiting for transfers between devices, exchange(): return lax.ppermute(block, ALL, route)  11.9 us
    pallas_call x1, Pallas kernels, per_device(): call(backward_kernel, [VM] * 9, [shaped(chunks, F32), shaped(chunks), sha...  8.41 us
    ppermute x10, waiting for transfers between devices, shift(): lax.ppermute(block, axis, [(i, (i + step) % count) for i in range(count)])  6.94 us
    pallas_call x1, Pallas kernels, per_device(): call(forward_kernel, [SM] + [VM] * 6, [shaped((TOK, D)), shaped((TOK, 128...  6.29 us
    pallas_call x1, Pallas kernels, per_device(): call(token_kernel, [VM] * 4, [shaped(full), shaped(whole), shaped(edge)],...  5.39 us
    pallas_call x1, Pallas kernels, per_device(): call(tok_halo_kernel, [VM, ANY], [shaped((22, 6, 2, D)), shaped((4, 6, 2,...  2.69 us
  transfers between devices with their start and end apart: 20, of which 7 were waited for; matrix products, arithmetic and copies ran while one was open for 0% of the time, Pallas kernels for 18%

profile of v1, /device:TPU:4, one launch (start us, length us, event | category | flops | bytes accessed | tf_op | source)
XLA Modules:
  0.0 92.0 jit_solution(7842066458825886196)
XLA Ops:
  0.6 2.7 %tok_halo.1 = (bf16[22,6,2,1024]{3,2,1,0:T(2,128)(2,1)}, bf16[4,6,2,1024]{3,2,1,0:T(2,128)(2,1)}, bf16[4,6,2,1024]{3,2,1,0:T(2,128)(2,1)}) custom-call(s32[12,24]{1,0:T(8,128)} %bitcast.2, bf16[24,12,2,1024]{3,2,1,0:T(2,128)(2,1)} %tok.3), custom_call_target="tpu_custom_call" | custom-call | bytes 8388608 | tf_op jit(solution)/shard_map/tok_halo/pallas_call | solution.py:404
  3.3 1.3 %collective-permute-start = (bf16[4,6,2,1024]{3,2,1,0:T(2,128)(2,1)}, bf16[4,6,2,1024]{3,2,1,0:T(2,128)(2,1)S(1)}, u32[]{:S(2)}, u32[]{:S(2)}) collective-permute-start(bf16[4,6,2,1024]{3,2,1,0:T(2,128)(2,1)} %get-tuple-element.61), channel_id=1, source_target_pairs={{0,1},{1,0},{2,3},{3,2},{4,5},{5,4},{6,7},{7,6},{8,9},{9,8},{10,11... | collective-permute-start | bytes 294920 | tf_op jit(solution)/shard_map/ppermute | solution.py:370
  4.6 2.8 %collective-permute-start.5 = (bf16[22,6,2,1024]{3,2,1,0:T(2,128)(2,1)}, bf16[22,6,2,1024]{3,2,1,0:T(2,128)(2,1)S(1)}, u32[]{:S(2)}, u32[]{:S(2)}) collective-permute-start(bf16[22,6,2,1024]{3,2,1,0:T(2,128)(2,1)} %get-tuple-element.71), channel_id=1, source_target_pairs={{0,254},{2,0},{4,2},{6,4},{8,6},{10,8},{12,10},{14,12},{16,14},{18... | collective-permute-start | bytes 1622024 | tf_op jit(solution)/shard_map/ppermute | solution.py:370
  7.4 1.9 %copy-done.2 = bf16[1024,1536]{1,0:T(8,128)(2,1)S(1)} copy-done((bf16[1024,1536]{1,0:T(8,128)(2,1)S(1)}, bf16[1024,1536]{1,0:T(8,128)(2,1)}, u32[]{:S(2)}) %copy-start.2) | copy-done | bytes 3145752
  9.3 0.3 weights.1
  9.7 0.0 collective-permute-done.lat
  9.7 0.2 cot_halo.1
  9.9 7.2 %collective-permute-start.2 = (bf16[21,6,2,1024]{3,2,1,0:T(2,128)(2,1)S(1)}, bf16[21,6,2,1024]{3,2,1,0:T(2,128)(2,1)S(1)}, u32[]{:S(2)}, u32[]{:S(2)}) collective-permute-start(bf16[21,6,2,1024]{3,2,1,0:T(2,128)(2,1)S(1)} %get-tuple-element.68), channel_id=1, source_target_pairs={{0,254},{2,0},{4,2},{6,4},{8,6},{10,8},{12,10},{14,12},{16,14},{18... | collective-permute-start | bytes 1548296 | tf_op jit(solution)/shard_map/ppermute | solution.py:370
  17.1 1.2 %collective-permute-start.3 = (bf16[3,6,2,1024]{3,2,1,0:T(2,128)(2,1)S(1)}, bf16[3,6,2,1024]{3,2,1,0:T(2,128)(2,1)S(1)}, u32[]{:S(2)}, u32[]{:S(2)}) collective-permute-start(bf16[3,6,2,1024]{3,2,1,0:T(2,128)(2,1)S(1)} %get-tuple-element.69), channel_id=1, source_target_pairs={{0,1},{1,0},{2,3},{3,2},{4,5},{5,4},{6,7},{7,6},{8,9},{9,8},{10,11... | collective-permute-start | bytes 221192 | tf_op jit(solution)/shard_map/ppermute | solution.py:370
  18.3 1.1 %collective-permute-start.4 = (bf16[3,6,2,1024]{3,2,1,0:T(2,128)(2,1)S(1)}, bf16[3,6,2,1024]{3,2,1,0:T(2,128)(2,1)S(1)}, u32[]{:S(2)}, u32[]{:S(2)}) collective-permute-start(bf16[3,6,2,1024]{3,2,1,0:T(2,128)(2,1)S(1)} %get-tuple-element.70), channel_id=1, source_target_pairs={{0,255},{1,254},{2,1},{3,0},{4,3},{5,2},{6,5},{7,4},{8,7},{9,6},{1... | collective-permute-start | bytes 221192 | tf_op jit(solution)/shard_map/ppermute | solution.py:378
  19.4 6.3 %forward.1 = (bf16[576,1024]{1,0:T(8,128)(2,1)S(1)}, f32[576,128]{1,0:T(8,128)S(1)}, bf16[576,1536]{1,0:T(8,128)(2,1)S(1)}, f32[4,4,2,144,144]{4,3,2,1,0:T(8,128...) custom-call(f32[8]{0:T(128)S(1)} %copy-done.5, bf16[24,12,2,1024]{3,2,1,0:T(2,128)(2,1)S(1)} %copy-done.1, ...), custom_call_target="tpu_custom_call" | custom-call | bytes 8388608 | tf_op jit(solution)/shard_map/forward/pallas_call | solution.py:441
  25.7 1.2 %collective-permute-done.3.lat = bf16[3,6,2,1024]{3,2,1,0:T(2,128)(2,1)S(1)} collective-permute-done((bf16[3,6,2,1024]{3,2,1,0:T(2,128)(2,1)S(1)}, bf16[3,6,2,1024]{3,2,1,0:T(2,128)(2,1)S(1)}, u32[]{:S(2)}, u32[]{:S(2)}) %collective-permute-start.3) | collective-permute-done | bytes 73760 | tf_op jit(solution)/shard_map/ppermute | solution.py:370
  27.0 0.0 collective-permute-done.4.diag
  27.0 0.0 collective-permute-done.2.main
  27.0 8.4 %backward.1 = (f32[32,16,2048]{2,1,0:T(8,128)S(1)}, bf16[32,16,2048]{2,1,0:T(8,128)(2,1)S(1)}, bf16[576,1536]{1,0:T(8,128)(2,1)S(1)}) custom-call(bf16[24,12,2,1024]{3,2,1,0:T(2,128)(2,1)S(1)} %copy-done, bf16[21,6,2,1024]{3,2,1,0:T(2,128)(2,1)S(1)} %collective-permute-done.2.main, bf16[3,6,2,1024]{3,2,1,0:T(2,128)(2,1)S(1)} %collective-permute-done.3.lat, ...), custom_call_target="tpu_custom_call" | custom-call | bytes 8388608 | tf_op jit(solution)/shard_map/backward/pallas_call | solution.py:458
  35.4 0.1 collective-permute-start.6
  35.5 0.5 collective-permute-start.7
  36.0 1.9 %out.1 = (bf16[24,12,2,1024]{3,2,1,0:T(2,128)(2,1)}, bf16[3,6,2,1024]{3,2,1,0:T(2,128)(2,1)S(1)}) custom-call(bf16[576,512]{1,0:T(8,128)(2,1)S(1)} %get-tuple-element.81.att, bf16[512,1024]{1,0:T(8,128)(2,1)S(1)} %get-tuple-element.79.wout), custom_call_target="tpu_custom_call" | custom-call | bytes 8388608 | tf_op jit(solution)/shard_map/out/pallas_call | solution.py:484
  37.9 1.8 %collective-permute-done.6.arrived = bf16[32,16,2048]{2,1,0:T(8,128)(2,1)S(1)} collective-permute-done((bf16[32,16,2048]{2,1,0:T(8,128)(2,1)S(1)}, bf16[32,16,2048]{2,1,0:T(8,128)(2,1)S(1)}, u32[]{:S(2)}, u32[]{:S(2)}) %collective-permute-start.6) | collective-permute-done | bytes 2097184 | tf_op jit(solution)/shard_map/ppermute | solution.py:370
  39.6 0.3 sum_core.1
  40.0 0.1 collective-permute-start.8
  40.1 1.0 %collective-permute-start.9 = (bf16[8,16,2048]{2,1,0:T(8,128)(2,1)S(1)}, bf16[8,16,2048]{2,1,0:T(8,128)(2,1)S(1)}, u32[]{:S(2)}, u32[]{:S(2)}) collective-permute-start(bf16[8,16,2048]{2,1,0:T(8,128)(2,1)S(1)} %get-tuple-element.97), channel_id=1, source_target_pairs={{0,8},{1,9},{2,26},{3,27},{4,12},{5,13},{6,30},{7,31},{8,0},{9,1},... | collective-permute-start | bytes 1572872 | tf_op jit(solution)/shard_map/ppermute | solution.py:396
  41.1 2.5 %collective-permute-start.10 = (bf16[8,16,2048]{2,1,0:T(8,128)(2,1)S(1)}, bf16[8,16,2048]{2,1,0:T(8,128)(2,1)S(1)}, u32[]{:S(2)}, u32[]{:S(2)}) collective-permute-start(bf16[8,16,2048]{2,1,0:T(8,128)(2,1)S(1)} %get-tuple-element.98), channel_id=1, source_target_pairs={{0,40},{1,41},{2,250},{3,251},{4,44},{5,45},{6,254},{7,255},{8,32}... | collective-permute-start | bytes 1572872 | tf_op jit(solution)/shard_map/ppermute | solution.py:396
  43.6 1.3 %collective-permute-done.7.att_left = bf16[4,72,512]{2,1,0:T(8,128)(2,1)S(1)} collective-permute-done((bf16[4,72,512]{2,1,0:T(8,128)(2,1)S(1)}, bf16[4,72,512]{2,1,0:T(8,128)(2,1)S(1)}, u32[]{:S(2)}, u32[]{:S(2)}) %collective-permute-start.7) | collective-permute-done | bytes 294944 | tf_op jit(solution)/shard_map/ppermute | solution.py:370
  44.9 5.4 %token_grad.1 = (bf16[24,12,2,1024]{3,2,1,0:T(2,128)(2,1)}, bf16[24,6,2,1024]{3,2,1,0:T(2,128)(2,1)S(1)}, bf16[3,6,2,1024]{3,2,1,0:T(2,128)(2,1)S(1)}) custom-call(bf16[576,1536]{1,0:T(8,128)(2,1)S(1)} %get-tuple-element.89.dqkv, bf16[1024,1536]{1,0:T(8,128)(2,1)S(1)} %get-tuple-element.74.wqkv, bf16[576,1024]{1,0:T(8,128)(2,1)S(1)} %get-tuple-element.75.nrm, ...), custom_call_target="tpu_custom_call" | custom-call | bytes 8388608 | tf_op jit(solution)/shard_map/token_grad/pallas_call | solution.py:497
  50.3 4.6 %collective-permute-start.14 = (bf16[24,6,2,1024]{3,2,1,0:T(2,128)(2,1)S(1)}, bf16[24,6,2,1024]{3,2,1,0:T(2,128)(2,1)S(1)}, u32[]{:S(2)}, u32[]{:S(2)}) collective-permute-start(bf16[24,6,2,1024]{3,2,1,0:T(2,128)(2,1)S(1)} %get-tuple-element.105), channel_id=1, source_target_pairs={{0,2},{2,4},{4,6},{6,8},{8,10},{10,12},{12,14},{14,16},{16,18},{18... | collective-permute-start | bytes 1769480 | tf_op jit(solution)/shard_map/ppermute | solution.py:370
  54.9 0.9 out_left.1.o_main
  55.7 0.0 collective-permute-done.8.a1
  55.8 0.0 collective-permute-done.9.a2
  55.8 0.0 collective-permute-done.10.a3
  55.8 0.3 sum_low.1
  56.0 1.9 %collective-permute-start.11 = (bf16[2,16,2048]{2,1,0:T(8,128)(2,1)S(1)}, bf16[2,16,2048]{2,1,0:T(8,128)(2,1)S(1)}, u32[]{:S(2)}, u32[]{:S(2)}) collective-permute-start(bf16[2,16,2048]{2,1,0:T(8,128)(2,1)S(1)} %get-tuple-element.100), channel_id=1, source_target_pairs={{0,64},{1,65},{2,66},{3,67},{4,68},{5,69},{6,70},{7,71},{8,72},{9,... | collective-permute-start | bytes 393224 | tf_op jit(solution)/shard_map/ppermute | solution.py:396
  57.9 6.2 %collective-permute-start.12 = (bf16[2,16,2048]{2,1,0:T(8,128)(2,1)S(1)}, bf16[2,16,2048]{2,1,0:T(8,128)(2,1)S(1)}, u32[]{:S(2)}, u32[]{:S(2)}) collective-permute-start(bf16[2,16,2048]{2,1,0:T(8,128)(2,1)S(1)} %get-tuple-element.101), channel_id=1, source_target_pairs={{0,24},{1,25},{2,10},{3,11},{4,28},{5,29},{6,14},{7,15},{8,16},{9,... | collective-permute-start | bytes 393224 | tf_op jit(solution)/shard_map/ppermute | solution.py:396
  64.1 0.0 collective-permute-done.11.a1
  64.1 2.9 %collective-permute-done.12.a2 = bf16[2,16,2048]{2,1,0:T(8,128)(2,1)S(1)} collective-permute-done((bf16[2,16,2048]{2,1,0:T(8,128)(2,1)S(1)}, bf16[2,16,2048]{2,1,0:T(8,128)(2,1)S(1)}, u32[]{:S(2)}, u32[]{:S(2)}) %collective-permute-start.12) | collective-permute-done | bytes 131104 | tf_op jit(solution)/shard_map/ppermute | solution.py:396
  67.1 6.7 %collective-permute-done.13.a3 = bf16[2,16,2048]{2,1,0:T(8,128)(2,1)S(1)} collective-permute-done((bf16[2,16,2048]{2,1,0:T(8,128)(2,1)S(1)}, bf16[2,16,2048]{2,1,0:T(8,128)(2,1)S(1)}, u32[]{:S(2)}, u32[]{:S(2)}) %collective-permute-start.13) | collective-permute-done | bytes 131104 | tf_op jit(solution)/shard_map/ppermute | solution.py:396
  73.8 0.1 sum_next.1
  73.9 0.0 collective-permute-done.14.t_main
  73.9 0.2 gather.1
  74.1 2.3 %collective-permute-start.15 = (bf16[2,3,12,2,1024]{4,3,2,1,0:T(2,128)(2,1)S(1)}, bf16[2,3,12,2,1024]{4,3,2,1,0:T(2,128)(2,1)S(1)}, u32[]{:S(2)}, u32[]{:S(2)}) collective-permute-start(bf16[2,3,12,2,1024]{4,3,2,1,0:T(2,128)(2,1)S(1)} %gather.1), channel_id=1, source_target_pairs={{0,1},{1,0},{2,3},{3,2},{4,5},{5,4},{6,7},{7,6},{8,9},{9,8},{10,11... | collective-permute-start | bytes 884744 | tf_op jit(solution)/shard_map/ppermute | solution.py:370
  76.4 4.9 %collective-permute-start.16 = (bf16[16,2048]{1,0:T(8,128)(2,1)S(1)}, bf16[16,2048]{1,0:T(8,128)(2,1)S(1)}, u32[]{:S(2)}, u32[]{:S(2)}) collective-permute-start(bf16[16,2048]{1,0:T(8,128)(2,1)S(1)} %get-tuple-element.110), channel_id=1, source_target_pairs={{0,192},{1,193},{2,194},{3,195},{4,196},{5,197},{6,198},{7,199},{8... | collective-permute-start | bytes 196616 | tf_op jit(solution)/shard_map/ppermute | solution.py:396
  81.2 2.2 %collective-permute-done.16.arrived = bf16[16,2048]{1,0:T(8,128)(2,1)S(1)} collective-permute-done((bf16[16,2048]{1,0:T(8,128)(2,1)S(1)}, bf16[16,2048]{1,0:T(8,128)(2,1)S(1)}, u32[]{:S(2)}, u32[]{:S(2)}) %collective-permute-start.16) | collective-permute-done | bytes 65568 | tf_op jit(solution)/shard_map/ppermute | solution.py:396
  83.5 0.2 collective-permute-start.17
  83.7 2.2 %collective-permute-start.19 = (bf16[16,1024]{1,0:T(8,128)(2,1)S(1)}, bf16[16,1024]{1,0:T(8,128)(2,1)S(1)}, u32[]{:S(2)}, u32[]{:S(2)}) collective-permute-start(bf16[16,1024]{1,0:T(8,128)(2,1)S(1)} %get-tuple-element.115), channel_id=1, source_target_pairs={{0,5},{1,4},{4,1},{5,0},{2,7},{3,6},{6,3},{7,2},{8,13},{9,12},{12,... | collective-permute-start | bytes 98312 | tf_op jit(solution)/shard_map/ppermute | solution.py:389
  85.9 1.8 %collective-permute-start.18 = (bf16[16,1024]{1,0:T(8,128)(2,1)S(1)}, bf16[16,1024]{1,0:T(8,128)(2,1)S(1)}, u32[]{:S(2)}, u32[]{:S(2)}) collective-permute-start(bf16[16,1024]{1,0:T(8,128)(2,1)S(1)} %get-tuple-element.115), channel_id=1, source_target_pairs={{0,4},{4,0},{1,5},{5,1},{2,6},{6,2},{3,7},{7,3},{8,12},{12,8},{9,1... | collective-permute-start | bytes 98312 | tf_op jit(solution)/shard_map/ppermute | solution.py:370
  87.7 1.1 %assemble.1 = (bf16[24,12,2,1024]{3,2,1,0:T(2,128)(2,1)}, bf16[24,12,2,1024]{3,2,1,0:T(2,128)(2,1)}) custom-call(bf16[24,12,2,1024]{3,2,1,0:T(2,128)(2,1)} %get-tuple-element.82.out_own, bf16[24,12,2,1024]{3,2,1,0:T(2,128)(2,1)} %get-tuple-element.91.tok_own, ...), custom_call_target="tpu_custom_call", output_to_operand_aliasing={{0}: (0, {}), {1}: (1, {})} | custom-call | bytes 8388608 | tf_op jit(solution)/shard_map/assemble/pallas_call | solution.py:536
  88.8 2.5 %collective-permute-done.18.a2 = bf16[16,1024]{1,0:T(8,128)(2,1)S(1)} collective-permute-done((bf16[16,1024]{1,0:T(8,128)(2,1)S(1)}, bf16[16,1024]{1,0:T(8,128)(2,1)S(1)}, u32[]{:S(2)}, u32[]{:S(2)}) %collective-permute-start.18) | collective-permute-done | bytes 32800 | tf_op jit(solution)/shard_map/ppermute | solution.py:370
  91.3 0.6 sum_x.1
  (19 shorter events, 0.1 us)
Async XLA Ops:
  0.6 6.8 %copy-start.3 = (bf16[512,1024]{1,0:T(8,128)(2,1)S(1)}, bf16[512,1024]{1,0:T(8,128)(2,1)}, u32[]{:S(2)}) copy-start(bf16[512,1024]{1,0:T(8,128)(2,1)} %wout_hbm) | copy-start | bytes 3145732
  3.3 6.3 %collective-permute-start = (bf16[4,6,2,1024]{3,2,1,0:T(2,128)(2,1)}, bf16[4,6,2,1024]{3,2,1,0:T(2,128)(2,1)S(1)}, u32[]{:S(2)}, u32[]{:S(2)}) collective-permute-start(bf16[4,6,2,1024]{3,2,1,0:T(2,128)(2,1)} %get-tuple-element.61), channel_id=1, source_target_pairs={{0,1},{1,0},{2,3},{3,2},{4,5},{5,4},{6,7},{7,6},{8,9},{9,8},{10,11... | collective-permute-start | bytes 294920 | tf_op jit(solution)/shard_map/ppermute | solution.py:370
  4.6 5.0 %collective-permute-start.1 = (bf16[4,6,2,1024]{3,2,1,0:T(2,128)(2,1)}, bf16[4,6,2,1024]{3,2,1,0:T(2,128)(2,1)S(1)}, u32[]{:S(2)}, u32[]{:S(2)}) collective-permute-start(bf16[4,6,2,1024]{3,2,1,0:T(2,128)(2,1)} %get-tuple-element.62), channel_id=1, source_target_pairs={{0,255},{1,254},{2,1},{3,0},{4,3},{5,2},{6,5},{7,4},{8,7},{9,6},{1... | collective-permute-start | bytes 294920 | tf_op jit(solution)/shard_map/ppermute | solution.py:378
  4.6 5.1 %copy-start = (bf16[24,12,2,1024]{3,2,1,0:T(2,128)(2,1)S(1)}, bf16[24,12,2,1024]{3,2,1,0:T(2,128)(2,1)}, u32[]{:S(2)}) copy-start(bf16[24,12,2,1024]{3,2,1,0:T(2,128)(2,1)} %cot.1) | copy-start | bytes 3538948
  4.6 14.8 %copy-start.1 = (bf16[24,12,2,1024]{3,2,1,0:T(2,128)(2,1)S(1)}, bf16[24,12,2,1024]{3,2,1,0:T(2,128)(2,1)}, u32[]{:S(2)}) copy-start(bf16[24,12,2,1024]{3,2,1,0:T(2,128)(2,1)} %tok.3) | copy-start | bytes 3538948
  4.6 14.8 %collective-permute-start.5 = (bf16[22,6,2,1024]{3,2,1,0:T(2,128)(2,1)}, bf16[22,6,2,1024]{3,2,1,0:T(2,128)(2,1)S(1)}, u32[]{:S(2)}, u32[]{:S(2)}) collective-permute-start(bf16[22,6,2,1024]{3,2,1,0:T(2,128)(2,1)} %get-tuple-element.71), channel_id=1, source_target_pairs={{0,254},{2,0},{4,2},{6,4},{8,6},{10,8},{12,10},{14,12},{16,14},{18... | collective-permute-start | bytes 1622024 | tf_op jit(solution)/shard_map/ppermute | solution.py:370
  7.4 1.9 %copy-start.2 = (bf16[1024,1536]{1,0:T(8,128)(2,1)S(1)}, bf16[1024,1536]{1,0:T(8,128)(2,1)}, u32[]{:S(2)}) copy-start(bf16[1024,1536]{1,0:T(8,128)(2,1)} %wqkv_hbm) | copy-start | bytes 9437188
  9.3 10.1 %copy-start.4 = (s32[24,12]{0,1:T(8,128)S(1)}, s32[24,12]{0,1:T(8,128)}, u32[]{:S(2)}) copy-start(s32[24,12]{0,1:T(8,128)} %param.7) | copy-start | bytes 3460
  9.3 10.1 %copy-start.5 = (f32[8]{0:T(128)S(1)}, f32[8]{0:T(128)}, u32[]{:S(2)}) copy-start(f32[8]{0:T(128)} %bias.1) | copy-start | bytes 100
  9.9 17.1 %collective-permute-start.2 = (bf16[21,6,2,1024]{3,2,1,0:T(2,128)(2,1)S(1)}, bf16[21,6,2,1024]{3,2,1,0:T(2,128)(2,1)S(1)}, u32[]{:S(2)}, u32[]{:S(2)}) collective-permute-start(bf16[21,6,2,1024]{3,2,1,0:T(2,128)(2,1)S(1)} %get-tuple-element.68), channel_id=1, source_target_pairs={{0,254},{2,0},{4,2},{6,4},{8,6},{10,8},{12,10},{14,12},{16,14},{18... | collective-permute-start | bytes 1548296 | tf_op jit(solution)/shard_map/ppermute | solution.py:370
  17.1 9.9 %collective-permute-start.3 = (bf16[3,6,2,1024]{3,2,1,0:T(2,128)(2,1)S(1)}, bf16[3,6,2,1024]{3,2,1,0:T(2,128)(2,1)S(1)}, u32[]{:S(2)}, u32[]{:S(2)}) collective-permute-start(bf16[3,6,2,1024]{3,2,1,0:T(2,128)(2,1)S(1)} %get-tuple-element.69), channel_id=1, source_target_pairs={{0,1},{1,0},{2,3},{3,2},{4,5},{5,4},{6,7},{7,6},{8,9},{9,8},{10,11... | collective-permute-start | bytes 221192 | tf_op jit(solution)/shard_map/ppermute | solution.py:370
  18.3 8.7 %collective-permute-start.4 = (bf16[3,6,2,1024]{3,2,1,0:T(2,128)(2,1)S(1)}, bf16[3,6,2,1024]{3,2,1,0:T(2,128)(2,1)S(1)}, u32[]{:S(2)}, u32[]{:S(2)}) collective-permute-start(bf16[3,6,2,1024]{3,2,1,0:T(2,128)(2,1)S(1)} %get-tuple-element.70), channel_id=1, source_target_pairs={{0,255},{1,254},{2,1},{3,0},{4,3},{5,2},{6,5},{7,4},{8,7},{9,6},{1... | collective-permute-start | bytes 221192 | tf_op jit(solution)/shard_map/ppermute | solution.py:378
  35.4 4.2 %collective-permute-start.6 = (bf16[32,16,2048]{2,1,0:T(8,128)(2,1)S(1)}, bf16[32,16,2048]{2,1,0:T(8,128)(2,1)S(1)}, u32[]{:S(2)}, u32[]{:S(2)}) collective-permute-start(bf16[32,16,2048]{2,1,0:T(8,128)(2,1)S(1)} %get-tuple-element.80), channel_id=1, source_target_pairs={{0,2},{2,0},{1,3},{3,1},{4,6},{6,4},{5,7},{7,5},{8,10},{10,8},{9,1... | collective-permute-start | bytes 6291464 | tf_op jit(solution)/shard_map/ppermute | solution.py:370
  35.5 9.4 %collective-permute-start.7 = (bf16[4,72,512]{2,1,0:T(8,128)(2,1)S(1)}, bf16[4,72,512]{2,1,0:T(8,128)(2,1)S(1)}, u32[]{:S(2)}, u32[]{:S(2)}) collective-permute-start(bf16[4,72,512]{2,1,0:T(8,128)(2,1)S(1)} %get-tuple-element.88), channel_id=1, source_target_pairs={{0,2},{2,4},{4,6},{6,8},{8,10},{10,12},{12,14},{14,16},{16,18},{18... | collective-permute-start | bytes 884744 | tf_op jit(solution)/shard_map/ppermute | solution.py:370
  40.0 15.7 %collective-permute-start.8 = (bf16[8,16,2048]{2,1,0:T(8,128)(2,1)S(1)}, bf16[8,16,2048]{2,1,0:T(8,128)(2,1)S(1)}, u32[]{:S(2)}, u32[]{:S(2)}) collective-permute-start(bf16[8,16,2048]{2,1,0:T(8,128)(2,1)S(1)} %get-tuple-element.96), channel_id=1, source_target_pairs={{0,32},{1,33},{2,226},{3,227},{4,36},{5,37},{6,230},{7,231},{8,40}... | collective-permute-start | bytes 1572872 | tf_op jit(solution)/shard_map/ppermute | solution.py:396
  40.1 15.7 %collective-permute-start.9 = (bf16[8,16,2048]{2,1,0:T(8,128)(2,1)S(1)}, bf16[8,16,2048]{2,1,0:T(8,128)(2,1)S(1)}, u32[]{:S(2)}, u32[]{:S(2)}) collective-permute-start(bf16[8,16,2048]{2,1,0:T(8,128)(2,1)S(1)} %get-tuple-element.97), channel_id=1, source_target_pairs={{0,8},{1,9},{2,26},{3,27},{4,12},{5,13},{6,30},{7,31},{8,0},{9,1},... | collective-permute-start | bytes 1572872 | tf_op jit(solution)/shard_map/ppermute | solution.py:396
  41.1 14.7 %collective-permute-start.10 = (bf16[8,16,2048]{2,1,0:T(8,128)(2,1)S(1)}, bf16[8,16,2048]{2,1,0:T(8,128)(2,1)S(1)}, u32[]{:S(2)}, u32[]{:S(2)}) collective-permute-start(bf16[8,16,2048]{2,1,0:T(8,128)(2,1)S(1)} %get-tuple-element.98), channel_id=1, source_target_pairs={{0,40},{1,41},{2,250},{3,251},{4,44},{5,45},{6,254},{7,255},{8,32}... | collective-permute-start | bytes 1572872 | tf_op jit(solution)/shard_map/ppermute | solution.py:396
  50.3 23.6 %collective-permute-start.14 = (bf16[24,6,2,1024]{3,2,1,0:T(2,128)(2,1)S(1)}, bf16[24,6,2,1024]{3,2,1,0:T(2,128)(2,1)S(1)}, u32[]{:S(2)}, u32[]{:S(2)}) collective-permute-start(bf16[24,6,2,1024]{3,2,1,0:T(2,128)(2,1)S(1)} %get-tuple-element.105), channel_id=1, source_target_pairs={{0,2},{2,4},{4,6},{6,8},{8,10},{10,12},{12,14},{14,16},{16,18},{18... | collective-permute-start | bytes 1769480 | tf_op jit(solution)/shard_map/ppermute | solution.py:370
  56.0 8.1 %collective-permute-start.11 = (bf16[2,16,2048]{2,1,0:T(8,128)(2,1)S(1)}, bf16[2,16,2048]{2,1,0:T(8,128)(2,1)S(1)}, u32[]{:S(2)}, u32[]{:S(2)}) collective-permute-start(bf16[2,16,2048]{2,1,0:T(8,128)(2,1)S(1)} %get-tuple-element.100), channel_id=1, source_target_pairs={{0,64},{1,65},{2,66},{3,67},{4,68},{5,69},{6,70},{7,71},{8,72},{9,... | collective-permute-start | bytes 393224 | tf_op jit(solution)/shard_map/ppermute | solution.py:396
  57.9 9.2 %collective-permute-start.12 = (bf16[2,16,2048]{2,1,0:T(8,128)(2,1)S(1)}, bf16[2,16,2048]{2,1,0:T(8,128)(2,1)S(1)}, u32[]{:S(2)}, u32[]{:S(2)}) collective-permute-start(bf16[2,16,2048]{2,1,0:T(8,128)(2,1)S(1)} %get-tuple-element.101), channel_id=1, source_target_pairs={{0,24},{1,25},{2,10},{3,11},{4,28},{5,29},{6,14},{7,15},{8,16},{9,... | collective-permute-start | bytes 393224 | tf_op jit(solution)/shard_map/ppermute | solution.py:396
  64.1 9.6 %collective-permute-start.13 = (bf16[2,16,2048]{2,1,0:T(8,128)(2,1)S(1)}, bf16[2,16,2048]{2,1,0:T(8,128)(2,1)S(1)}, u32[]{:S(2)}, u32[]{:S(2)}) collective-permute-start(bf16[2,16,2048]{2,1,0:T(8,128)(2,1)S(1)} %get-tuple-element.102), channel_id=1, source_target_pairs={{0,88},{1,89},{2,74},{3,75},{4,92},{5,93},{6,78},{7,79},{8,80},{9,... | collective-permute-start | bytes 393224 | tf_op jit(solution)/shard_map/ppermute | solution.py:396
  74.1 13.6 %collective-permute-start.15 = (bf16[2,3,12,2,1024]{4,3,2,1,0:T(2,128)(2,1)S(1)}, bf16[2,3,12,2,1024]{4,3,2,1,0:T(2,128)(2,1)S(1)}, u32[]{:S(2)}, u32[]{:S(2)}) collective-permute-start(bf16[2,3,12,2,1024]{4,3,2,1,0:T(2,128)(2,1)S(1)} %gather.1), channel_id=1, source_target_pairs={{0,1},{1,0},{2,3},{3,2},{4,5},{5,4},{6,7},{7,6},{8,9},{9,8},{10,11... | collective-permute-start | bytes 884744 | tf_op jit(solution)/shard_map/ppermute | solution.py:370
  76.4 7.1 %collective-permute-start.16 = (bf16[16,2048]{1,0:T(8,128)(2,1)S(1)}, bf16[16,2048]{1,0:T(8,128)(2,1)S(1)}, u32[]{:S(2)}, u32[]{:S(2)}) collective-permute-start(bf16[16,2048]{1,0:T(8,128)(2,1)S(1)} %get-tuple-element.110), channel_id=1, source_target_pairs={{0,192},{1,193},{2,194},{3,195},{4,196},{5,197},{6,198},{7,199},{8... | collective-permute-start | bytes 196616 | tf_op jit(solution)/shard_map/ppermute | solution.py:396
  83.5 5.3 %collective-permute-start.17 = (bf16[16,1024]{1,0:T(8,128)(2,1)S(1)}, bf16[16,1024]{1,0:T(8,128)(2,1)S(1)}, u32[]{:S(2)}, u32[]{:S(2)}) collective-permute-start(bf16[16,1024]{1,0:T(8,128)(2,1)S(1)} %get-tuple-element.114.keep), channel_id=1, source_target_pairs={{0,1},{1,0},{2,3},{3,2},{4,5},{5,4},{6,7},{7,6},{8,9},{9,8},{10,11... | collective-permute-start | bytes 98312 | tf_op jit(solution)/shard_map/ppermute | solution.py:370
  83.7 5.1 %collective-permute-start.19 = (bf16[16,1024]{1,0:T(8,128)(2,1)S(1)}, bf16[16,1024]{1,0:T(8,128)(2,1)S(1)}, u32[]{:S(2)}, u32[]{:S(2)}) collective-permute-start(bf16[16,1024]{1,0:T(8,128)(2,1)S(1)} %get-tuple-element.115), channel_id=1, source_target_pairs={{0,5},{1,4},{4,1},{5,0},{2,7},{3,6},{6,3},{7,2},{8,13},{9,12},{12,... | collective-permute-start | bytes 98312 | tf_op jit(solution)/shard_map/ppermute | solution.py:389
  85.9 5.4 %collective-permute-start.18 = (bf16[16,1024]{1,0:T(8,128)(2,1)S(1)}, bf16[16,1024]{1,0:T(8,128)(2,1)S(1)}, u32[]{:S(2)}, u32[]{:S(2)}) collective-permute-start(bf16[16,1024]{1,0:T(8,128)(2,1)S(1)} %get-tuple-element.115), channel_id=1, source_target_pairs={{0,4},{4,0},{1,5},{5,1},{2,6},{6,2},{3,7},{7,3},{8,12},{12,8},{9,1... | collective-permute-start | bytes 98312 | tf_op jit(solution)/shard_map/ppermute | solution.py:370
